TPU v7x, 32 devices: a whole 2x2x4 slice. The times are simulated.
32 devices in a mesh: seq: 8 (over z, y), head: 4 (over x, core).
Axes of the slice: x: 2, y: 2, z: 4, core: 2. Of those that a mesh axis runs over, the one named last changes fastest.
Arguments:
- block_input: float32 [2, 4096, 1024], P(None, 'seq'), may hold values from -6 to 6
- attn_gain: float32 [1024], replicated, may hold values from 0.5 to 1.5
- query_weight: bfloat16 [1024, 512], P(None, 'head'), may hold values from -0.1875 to 0.1875
- key_weight: bfloat16 [1024, 512], P(None, 'head'), may hold values from -0.1875 to 0.1875
- value_weight: bfloat16 [1024, 1024], P(None, 'head'), may hold values from -0.1875 to 0.1875
- gate_weight: bfloat16 [1024, 1024], P(None, 'head'), may hold values from -0.1875 to 0.1875
- decay_down: bfloat16 [1024, 16], replicated, may hold values from -0.1875 to 0.1875
- decay_up: bfloat16 [16, 512], P(None, 'head'), may hold values from -0.75 to 0.75
- decay_bias: float32 [512], P('head'), may hold values from -3 to 10
- query_conv: float32 [4, 512], P(None, 'head'), may hold values from -3 to 3
- key_conv: float32 [4, 512], P(None, 'head'), may hold values from -3 to 3
- value_conv: float32 [4, 1024], P(None, 'head'), may hold values from -3 to 3
- head_gain: float32 [256], replicated, may hold values from 0.5 to 1.5
- out_weight: bfloat16 [1024, 1024], P('head'), may hold values from -0.375 to 0.375
- ffn_gain: float32 [1024], replicated, may hold values from 0.5 to 1.5
- ffn_gate: bfloat16 [1024, 2816], P(None, 'head'), may hold values from -0.1875 to 0.1875
- ffn_up: bfloat16 [1024, 2816], P(None, 'head'), may hold values from -0.1875 to 0.1875
- ffn_down: bfloat16 [2816, 1024], P('head'), may hold values from -0.109375 to 0.109375
- out_grad: float32 [2, 4096, 1024], P(None, 'seq'), may hold values from -6 to 6
Outputs:
- block_output: float32 [2, 4096, 1024], P(None, 'seq')
- input_grad: float32 [2, 4096, 1024], P(None, 'seq')
- attn_gain_grad: float32 [1024], replicated
- query_weight_grad: float32 [1024, 512], P(None, 'head')
- key_weight_grad: float32 [1024, 512], P(None, 'head')
- value_weight_grad: float32 [1024, 1024], P(None, 'head')
- gate_weight_grad: float32 [1024, 1024], P(None, 'head')
- decay_down_grad: float32 [1024, 16], replicated
- decay_up_grad: float32 [16, 512], P(None, 'head')
- decay_bias_grad: float32 [512], P('head')
- query_conv_grad: float32 [4, 512], P(None, 'head')
- key_conv_grad: float32 [4, 512], P(None, 'head')
- value_conv_grad: float32 [4, 1024], P(None, 'head')
- head_gain_grad: float32 [256], replicated
- out_weight_grad: float32 [1024, 1024], P('head')
- ffn_gain_grad: float32 [1024], replicated
- ffn_gate_grad: float32 [1024, 2816], P(None, 'head')
- ffn_up_grad: float32 [1024, 2816], P(None, 'head')
- ffn_down_grad: float32 [2816, 1024], P('head')
All inputs are finite; a program needn't handle non-finite values.
Results may differ from a plain program's by a relative error of at most 0.0075.
The roundings to bfloat16 on the way count: a program that leaves them out, or rounds other values in their place, can miss the bound.
Values sent between devices are 32-bit elements; how exact they have to be, the bound alone decides.
A program may use at most 192 MiB of HBM per device.

v0:
```python
import jax
import jax.numpy as jnp
from jax import lax
from jax.sharding import PartitionSpec as P

GROUP = 64


EPS = 1e-06
HIGH = lax.Precision.HIGHEST


def shifted(value, axis, steps):
    count = lax.axis_size(axis)
    initial, last = (max(0, -steps), min(count, count - steps))
    return lax.ppermute(value, axis, [(source, source + steps) for source in range(initial, last)])


def carried_in(part, axis, combine, identity, reverse):
    count = lax.axis_size(axis)
    place = lax.axis_index(axis)
    ahead = count - 1 - place if reverse else place
    gathered = jax.tree.map(lambda a: lax.all_gather(a, axis), part)
    state = jax.tree.map(lambda a, e: jnp.zeros_like(a) + jnp.asarray(e, a.dtype), part, identity)

    def one(turn, state):
        source = count - 1 - turn if reverse else turn
        return combine(
            state, jax.tree.map(lambda a: lax.dynamic_index_in_dim(a, source, 0, False), gathered)
        )

    return lax.fori_loop(0, ahead, one, state)


def rms_scale(values):
    return lax.rsqrt(jnp.mean(values * values, axis=-1, keepdims=True) + EPS)


def rms_back(grad_normed, normed, scale):
    return scale * (grad_normed - normed * jnp.mean(grad_normed * normed, axis=-1, keepdims=True))


def silu_slope(values):
    sigma = jax.nn.sigmoid(values)
    return sigma * (1.0 + values * (1.0 - sigma))


def half_dot(left, right):
    return jnp.dot(left, right, preferred_element_type=jnp.float32)


def half_outer(left, right):
    return lax.dot_general(
        left, right, (((0,), (0,)), ((), ())), preferred_element_type=jnp.float32
    )


def half_back(left, right):
    return lax.dot_general(
        left, right, (((1,), (1,)), ((), ())), preferred_element_type=jnp.float32
    )


def exact_dot(left, right):
    return jnp.dot(left, right, precision=HIGH, preferred_element_type=jnp.float32)


def exact_outer(left, right):
    return lax.dot_general(
        left, right, (((0,), (0,)), ((), ())), precision=HIGH, preferred_element_type=jnp.float32
    )


def exact_back(left, right):
    return lax.dot_general(
        left, right, (((1,), (1,)), ((), ())), precision=HIGH, preferred_element_type=jnp.float32
    )


def group_step(state, pieces):
    queries, key_rows, value_rows, decay_log = pieces
    inner = jnp.cumsum(decay_log, axis=1)
    count = inner.shape[1]
    lower = (jnp.arange(count)[:, None] >= jnp.arange(count)[None, :])[None, :, :, None]
    spread = inner[:, :, None, :] - inner[:, None, :, :]
    factors = jnp.exp(jnp.where(lower, spread, 0.0)) * lower.astype(jnp.float32)
    scores = jnp.einsum("btd,bsd,btsd->bts", queries, key_rows, factors, precision=HIGH)
    output = jnp.einsum("bts,bsv->btv", scores, value_rows, precision=HIGH)
    output = output + jnp.einsum("btk,bkv->btv", queries * jnp.exp(inner), state, precision=HIGH)
    last_row = inner[:, -1, :]
    carried = jnp.einsum(
        "bsk,bsv->bkv", key_rows * jnp.exp(last_row[:, None, :] - inner), value_rows, precision=HIGH
    )
    state = jnp.exp(last_row)[:, :, None] * state + carried
    return (state, output)


def group_scan(queries, key_rows, value_rows, decay_log, state, group_len):
    count = queries.shape[1]

    def split(values):
        return jnp.moveaxis(
            values.reshape(values.shape[0], count // group_len, group_len, values.shape[2]), 1, 0
        )

    state, output = lax.scan(
        jax.checkpoint(group_step),
        state,
        (split(queries), split(key_rows), split(value_rows), split(decay_log)),
    )
    output = jnp.moveaxis(output, 0, 1).reshape(queries.shape[0], count, value_rows.shape[2])
    return (output, state)


def link_states(earlier, later):
    return (earlier[0] * later[0], later[0][:, :, None] * earlier[1] + later[1])


def shards(
    block_input,
    attn_gain,
    query_weight,
    key_weight,
    value_weight,
    gate_weight,
    decay_down,
    decay_up,
    decay_bias,
    query_conv,
    key_conv,
    value_conv,
    head_gain,
    out_weight,
    ffn_gain,
    ffn_gate,
    ffn_up,
    ffn_down,
    out_grad,
):
    seq_count, tok_rows, model_width = block_input.shape
    key_size = query_weight.shape[1]
    value_size = value_weight.shape[1]
    taps = query_conv.shape[0]
    row_count = seq_count * tok_rows
    inputs = block_input.reshape(row_count, model_width)
    scale_one = rms_scale(inputs)
    normed_one = inputs * scale_one
    hidden_one = (normed_one * attn_gain).astype(jnp.bfloat16)
    query_raw = half_dot(hidden_one, query_weight)
    key_raw = half_dot(hidden_one, key_weight)
    value_raw = half_dot(hidden_one, value_weight)
    gate_raw = half_dot(hidden_one, gate_weight)
    hidden_wide = hidden_one.astype(jnp.float32)
    down_wide = decay_down.astype(jnp.float32)
    up_wide = decay_up.astype(jnp.float32)
    rank_rows = exact_dot(hidden_wide, down_wide)
    decay_pre = exact_dot(rank_rows, up_wide) + decay_bias
    decay_log = (jax.nn.log_sigmoid(decay_pre) / 16.0).reshape(seq_count, tok_rows, key_size)
    conv_in = jnp.concatenate([query_raw, key_raw, value_raw], axis=1).reshape(
        seq_count, tok_rows, 2 * key_size + value_size
    )
    conv_weight = jnp.concatenate([query_conv, key_conv, value_conv], axis=1)
    edge_rows = shifted(conv_in[:, tok_rows - (taps - 1) :], "seq", 1)
    padded = jnp.concatenate([edge_rows, conv_in], axis=1)
    conv_pre = jnp.zeros_like(conv_in)
    for offset in range(taps):
        conv_pre = conv_pre + conv_weight[offset] * padded[:, offset : offset + tok_rows]
    conv_out = jax.nn.silu(conv_pre)
    factor = key_size ** (-0.5)
    queries = conv_out[:, :, :key_size] * factor
    key_rows = conv_out[:, :, key_size : 2 * key_size]
    value_rows = conv_out[:, :, 2 * key_size :]
    zero_state = jnp.zeros((seq_count, key_size, value_size), jnp.float32)
    local_out, local_state = group_scan(queries, key_rows, value_rows, decay_log, zero_state, GROUP)
    running = jnp.cumsum(decay_log, axis=1)
    query_decayed = queries * jnp.exp(running)
    block_decay = jnp.exp(running[:, -1])
    unit_decay = jnp.ones_like(block_decay)
    prior, state_in = carried_in(
        (block_decay, local_state), "seq", link_states, (unit_decay, zero_state), False
    )
    mixed_rows = local_out + jnp.einsum("btk,bkv->btv", query_decayed, state_in, precision=HIGH)
    mixed_rows = mixed_rows.reshape(row_count, value_size)
    head_scale = rms_scale(mixed_rows)
    head_normed = mixed_rows * head_scale
    normed_gain = head_normed * head_gain
    gate_act = jax.nn.silu(gate_raw)
    gated_rows = (normed_gain * gate_act).astype(jnp.bfloat16)
    mixer_out = lax.psum(half_dot(gated_rows, out_weight), "head")
    middle = inputs + mixer_out
    scale_two = rms_scale(middle)
    normed_two = middle * scale_two
    hidden_two = (normed_two * ffn_gain).astype(jnp.bfloat16)
    gate_rows = half_dot(hidden_two, ffn_gate)
    up_rows = half_dot(hidden_two, ffn_up)
    inner_rows = (jax.nn.silu(gate_rows) * up_rows).astype(jnp.bfloat16)
    ffn_out = lax.psum(half_dot(inner_rows, ffn_down), "head")
    block_output = (middle + ffn_out).reshape(seq_count, tok_rows, model_width)
    grad_rows = out_grad.reshape(row_count, model_width)
    grad_ffn = grad_rows.astype(jnp.bfloat16)
    ffn_down_grad = half_outer(inner_rows, grad_ffn)
    grad_inner = half_back(grad_ffn, ffn_down)
    grad_up = (grad_inner * jax.nn.silu(gate_rows)).astype(jnp.bfloat16)
    grad_gate = (grad_inner * up_rows * silu_slope(gate_rows)).astype(jnp.bfloat16)
    ffn_gate_grad = half_outer(hidden_two, grad_gate)
    ffn_up_grad = half_outer(hidden_two, grad_up)
    grad_hidden_two = lax.psum(half_back(grad_gate, ffn_gate) + half_back(grad_up, ffn_up), "head")
    ffn_gain_grad = jnp.sum(grad_hidden_two * normed_two, axis=0)
    grad_middle = grad_rows + rms_back(grad_hidden_two * ffn_gain, normed_two, scale_two)
    grad_mixer = grad_middle.astype(jnp.bfloat16)
    out_weight_grad = half_outer(gated_rows, grad_mixer)
    grad_gated = half_back(grad_mixer, out_weight)
    grad_normed = grad_gated * gate_act
    grad_gate_raw = (grad_gated * normed_gain * silu_slope(gate_raw)).astype(jnp.bfloat16)
    head_gain_part = jnp.sum(grad_normed * head_normed, axis=0)
    grad_mixed = rms_back(grad_normed * head_gain, head_normed, head_scale).reshape(
        seq_count, tok_rows, value_size
    )
    state_pull = jnp.einsum("btk,btv->bkv", query_decayed, grad_mixed, precision=HIGH)
    later, grad_state_out = carried_in(
        (block_decay, state_pull), "seq", link_states, (unit_decay, zero_state), True
    )

    def attend(query_part, key_part, value_part, decay_part):
        return group_scan(query_part, key_part, value_part, decay_part, state_in, GROUP)

    unused, attend_back = jax.vjp(attend, queries, key_rows, value_rows, decay_log)
    grad_queries, grad_keys, grad_values, grad_decay = attend_back((grad_mixed, grad_state_out))
    grad_conv_out = jnp.concatenate([grad_queries * factor, grad_keys, grad_values], axis=2)
    grad_conv_pre = grad_conv_out * silu_slope(conv_pre)
    grad_padded = jnp.zeros_like(padded)
    tap_grads = []
    for offset in range(taps):
        grad_padded = grad_padded + jnp.pad(
            conv_weight[offset] * grad_conv_pre, ((0, 0), (offset, taps - 1 - offset), (0, 0))
        )
        tap_grads.append(
            jnp.sum(padded[:, offset : offset + tok_rows] * grad_conv_pre, axis=(0, 1))
        )
    conv_grad = jnp.stack(tap_grads)
    edge_back = shifted(grad_padded[:, : taps - 1], "seq", -1)
    grad_conv_in = grad_padded[:, taps - 1 :] + jnp.pad(
        edge_back, ((0, 0), (tok_rows - taps + 1, 0), (0, 0))
    )
    grad_in_rows = grad_conv_in.reshape(row_count, 2 * key_size + value_size).astype(jnp.bfloat16)
    grad_query_raw = grad_in_rows[:, :key_size]
    grad_key_raw = grad_in_rows[:, key_size : 2 * key_size]
    grad_value_raw = grad_in_rows[:, 2 * key_size :]
    grad_pre = grad_decay.reshape(row_count, key_size) / 16.0 * jax.nn.sigmoid(-decay_pre)
    decay_bias_grad = jnp.sum(grad_pre, axis=0)
    decay_up_grad = exact_outer(rank_rows, grad_pre)
    grad_rank = exact_back(grad_pre, up_wide)
    decay_down_part = exact_outer(hidden_wide, grad_rank)
    query_weight_grad = half_outer(hidden_one, grad_query_raw)
    key_weight_grad = half_outer(hidden_one, grad_key_raw)
    value_weight_grad = half_outer(hidden_one, grad_value_raw)
    gate_weight_grad = half_outer(hidden_one, grad_gate_raw)
    hidden_part = half_back(grad_query_raw, query_weight) + half_back(grad_key_raw, key_weight)
    hidden_part = (
        hidden_part
        + half_back(grad_value_raw, value_weight)
        + half_back(grad_gate_raw, gate_weight)
    )
    hidden_part = hidden_part + exact_back(grad_rank, down_wide)
    grad_hidden_one = lax.psum(hidden_part, "head")
    attn_gain_grad = jnp.sum(grad_hidden_one * normed_one, axis=0)
    input_grad = (
        grad_middle + rms_back(grad_hidden_one * attn_gain, normed_one, scale_one)
    ).reshape(seq_count, tok_rows, model_width)
    decay_down_grad, head_gain_grad = lax.psum((decay_down_part, head_gain_part), ("seq", "head"))
    (
        attn_gain_grad,
        query_weight_grad,
        key_weight_grad,
        value_weight_grad,
        gate_weight_grad,
        decay_up_grad,
        decay_bias_grad,
        conv_grad,
        out_weight_grad,
        ffn_gain_grad,
        ffn_gate_grad,
        ffn_up_grad,
        ffn_down_grad,
    ) = lax.psum(
        (
            attn_gain_grad,
            query_weight_grad,
            key_weight_grad,
            value_weight_grad,
            gate_weight_grad,
            decay_up_grad,
            decay_bias_grad,
            conv_grad,
            out_weight_grad,
            ffn_gain_grad,
            ffn_gate_grad,
            ffn_up_grad,
            ffn_down_grad,
        ),
        "seq",
    )
    query_conv_grad = conv_grad[:, :key_size]
    key_conv_grad = conv_grad[:, key_size : 2 * key_size]
    value_conv_grad = conv_grad[:, 2 * key_size :]
    return (
        block_output,
        input_grad,
        attn_gain_grad,
        query_weight_grad,
        key_weight_grad,
        value_weight_grad,
        gate_weight_grad,
        decay_down_grad,
        decay_up_grad,
        decay_bias_grad,
        query_conv_grad,
        key_conv_grad,
        value_conv_grad,
        head_gain_grad,
        out_weight_grad,
        ffn_gain_grad,
        ffn_gate_grad,
        ffn_up_grad,
        ffn_down_grad,
    )


def solution(mesh):
    in_specs = (
        P(None, "seq", None),
        P(),
        P(None, "head"),
        P(None, "head"),
        P(None, "head"),
        P(None, "head"),
        P(),
        P(None, "head"),
        P("head"),
        P(None, "head"),
        P(None, "head"),
        P(None, "head"),
        P(),
        P("head", None),
        P(),
        P(None, "head"),
        P(None, "head"),
        P("head", None),
        P(None, "seq", None),
    )
    out_specs = (
        P(None, "seq", None),
        P(None, "seq", None),
        P(),
        P(None, "head"),
        P(None, "head"),
        P(None, "head"),
        P(None, "head"),
        P(),
        P(None, "head"),
        P("head"),
        P(None, "head"),
        P(None, "head"),
        P(None, "head"),
        P(),
        P("head", None),
        P(),
        P(None, "head"),
        P(None, "head"),
        P("head", None),
    )
    return jax.shard_map(shards, mesh=mesh, in_specs=in_specs, out_specs=out_specs, check_vma=False)
```

profile of v0, /device:TPU:0, one launch (start us, length us, event | category | flops | bytes accessed | tf_op | source)
XLA Modules:
  0.0 1432.1 jit_solution(1660719305530751324)
XLA Ops:
  16.0 2.9 copy.147
  20.3 4.9 collective-permute-start
  32.2 5.5 fusion.52
  41.8 130.7 %while.77 = (s32[]{:T(128)}, f32[2,128,256]{2,1,0:T(8,128)}, f32[8,2,64,256]{3,2,1,0:T(8,128)}, f32[8,2,64,128]{3,2,1,0:T(8,128)}, f32[8,2,64,128]{3,2,1,0:T(8,1...) while((s32[]{:T(128)}, f32[2,128,256]{2,1,0:T(8,128)}, ...), condition=%wide.region_3.4_spmd.clone, body=%wide.region_1.3_spmd.clone.sunk | while | flops 133496832 | bytes 11223704 | solution.py:106
  47.8 4.2 fusion.217
  63.9 4.2 fusion.217
  80.3 4.2 fusion.217
  96.6 4.2 fusion.217
  113.0 4.2 fusion.217
  129.4 4.2 fusion.217
  145.8 4.2 fusion.217
  162.2 4.2 fusion.217
  180.3 19.5 %all-gather = f32[16,1,128]{2,1,0:T(1,128)} all-gather(f32[2,1,128]{2,1,0:T(1,128)S(1)} %slice_exponential_fusion), channel_id=2, replica_groups=mesh['seq'=8,'head'=4] {'seq'}, dimensions={0}, use_global_device_ids=true | all-gather | bytes 9216 | tf_op jit(solution)/shard_map/all_gather | solution.py:23
  202.0 20.4 %all-gather.6.cloned.1.call-done = f32[16,128,256]{2,1,0:T(8,128)} async-done(((f32[2,128,256]{2,1,0:T(8,128)}), f32[16,128,256]{2,1,0:T(8,128)}) %all-gather.6.cloned.1.call-update) | async-done | bytes 2097168 | tf_op jit(solution)/shard_map/all_gather | solution.py:23
  223.2 2.9 multiply_reduce_fusion.13
  231.6 3.9 bitcast_convert_fusion
  235.5 97.6 %all-reduce.15.cloned.1.call-done = f32[1024,1024]{1,0:T(8,128)} async-done(((f32[1024,1024]{1,0:T(8,128)}), f32[1024,1024]{1,0:T(8,128)}) %all-reduce.15.cloned.1.call-update) | async-done | bytes 4194320 | tf_op jit(solution)/shard_map/psum | solution.py:189
  333.1 4.0 multiply_reduce_fusion.5
  343.5 3.9 multiply_convert_fusion.2
  349.2 3.9 convolution_add_fusion.5
  353.6 85.3 %all-reduce.17.cloned.1.call-done = f32[1024,1024]{1,0:T(8,128)} async-done(((f32[1024,1024]{1,0:T(8,128)}), f32[1024,1024]{1,0:T(8,128)}) %all-reduce.17.cloned.1.call-update) | async-done | bytes 4194320 | tf_op jit(solution)/shard_map/psum | solution.py:207
  439.0 5.3 multiply_reduce_fusion.1
  445.0 3.2 bitcast_add_fusion.4
  455.5 61.2 %while.75 = (s32[]{:T(128)}, f32[2,128,256]{2,1,0:T(8,128)}, f32[8,2,128,256]{3,2,1,0:T(8,128)}, f32[8,2,64,128]{3,2,1,0:T(8,128)}, f32[8,2,64,128]{3,2,1,0:T(8,...) while((s32[]{:T(128)}, f32[2,128,256]{2,1,0:T(8,128)}, f32[8,2,128,256]{3,2,1,0:T(8,128)}, ...), condition=%wide.region_19.20_spmd, body=%wide.region_17.19_spmd.sunk | while | flops 51527680 | bytes 1580637 | solution.py:106
  516.7 5.3 fusion.88
  526.4 12.3 while.74
  542.4 148.9 %while.76 = (s32[]{:T(128)}, f32[2,128,256]{2,1,0:T(8,128)S(1)}, f32[8,2,64,128]{3,2,0,1:T(8,128)}, f32[8,2,64,128]{3,2,0,1:T(8,128)}, f32[8,2,64,256]{3,2,0,1:T...) while((s32[]{:T(128)}, f32[2,128,256]{2,1,0:T(8,128)S(1)}, ...), condition=%wide.region_27.28_spmd, body=%wide.region_20.27_spmd.sunk | while | flops 279494656 | bytes 7372989 | solution.py:106
  553.7 4.3 fusion.209
  572.4 4.3 fusion.209
  591.0 4.3 fusion.209
  609.6 4.3 fusion.209
  628.2 4.3 fusion.209
  646.9 4.3 fusion.209
  665.5 4.3 fusion.209
  684.1 4.3 fusion.209
  692.5 6.1 multiply_reduce_fusion.10
  710.0 4.8 add_add_fusion
  715.1 5.8 fusion.96
  720.9 3.2 fusion.97
  724.2 3.2 fusion.95
  739.0 38.7 %psum.146 = f32[256]{0:T(256)} all-reduce(f32[256]{0:T(256)S(1)} %copy-done.72), channel_id=1, replica_groups=mesh['seq'=8,'head'=4] {'seq','head'}, use_global_device_ids=true, to_apply=%region_46.47 | all-reduce | flops 256 | bytes 2048 | tf_op jit(solution)/shard_map/psum | solution.py:270
  778.1 88.0 %all-reduce.23.cloned.1.call-done = (f32[1024,1024]{1,0:T(8,128)}, f32[1024,1024]{1,0:T(8,128)}) async-done(((f32[1024,1024]{1,0:T(8,128)}, f32[1024,1024]{1,0:T(8,128)}), (f32[1024,1024]{1,0:T(8,128)}, f32[1024,1024]{1,0:T(8,128)})) %all-reduce.23.cloned.1.call-update) | async-done | bytes 8388624 | tf_op jit(solution)/shard_map/psum | solution.py:197
  866.1 4.6 multiply_reduce_fusion.2
  870.7 38.2 %all-reduce.6 = (f32[1024]{0:T(1024)}, f32[16,128]{1,0:T(8,128)}, f32[128]{0:T(128)}, f32[4,512]{1,0:T(4,128)S(1)}, f32[1024]{0:T(1024)}) all-reduce(f32[1024]{0:T(1024)S(1)} %get-tuple-element.576, f32[16,128]{1,0:T(8,128)S(1)} %fusion.94, f32[128]{0:T(128)S(1)} %get-tuple-element.670, ...), channel_id=1, replica_groups=mesh['seq'=8,'head'=4] {'seq'}, use_global_device_ids=true, to_apply=%region_31.32 | all-reduce | flops 6272 | bytes 50176 | tf_op jit(solution)/shard_map/psum | solution.py:285
  909.5 7.1 add.252
  918.2 2.9 multiply_add_fusion.1
  921.1 68.1 %all-reduce.19.cloned.1.call-done = f32[1024,16]{0,1:T(8,128)} async-done(((f32[1024,16]{0,1:T(8,128)}), f32[1024,16]{0,1:T(8,128)}) %all-reduce.19.cloned.1.call-update) | async-done | bytes 65552 | tf_op jit(solution)/shard_map/psum | solution.py:270
  989.2 420.9 %all-reduce.21.cloned.1.call-done = (f32[1024,128]{1,0:T(8,128)}, f32[1024,128]{1,0:T(8,128)}, f32[1024,256]{1,0:T(8,128)}, f32[1024,256]{1,0:T(8,128)}, f32[256...) async-done(((f32[1024,128]{1,0:T(8,128)}, f32[1024,128]{1,0:T(8,128)}, f32[1024,256]{1,0:T(8,128)}, f32[1024,256]{1,0:T(8,128)}, ...) | async-done | bytes 12845072 | tf_op jit(solution)/shard_map/psum | solution.py:285
  (601 shorter events, 387.6 us)
Async XLA Ops:
  7.2 336.2 %copy-start = (bf16[704,1024]{1,0:T(8,128)(2,1)S(1)}, bf16[704,1024]{1,0:T(8,128)(2,1)}, u32[]{:S(2)}) copy-start(bf16[704,1024]{1,0:T(8,128)(2,1)} %param.46) | copy-start | bytes 4325380
  7.2 215.2 %all-gather.6.cloned.1.call-start = ((), (), s32[]{:S(2)}) async-start(), calls=%async_computation.3 | async-start | bytes 2359296 | tf_op jit(solution)/shard_map/all_gather | solution.py:23
  7.3 3.5 copy-start.2
  18.9 8.4 copy-start.71
  18.9 8.4 copy-start.70
  18.9 9.0 copy-start.68
  18.9 9.0 copy-start.77
  20.3 11.9 collective-permute-start
  172.5 160.6 %all-reduce.15.cloned.1.call-start = ((), (), s32[]{:S(2)}) async-start(), calls=%async_computation | async-start | bytes 8388608 | tf_op jit(solution)/shard_map/psum | solution.py:189
  223.2 3.0 copy-start.46
  223.2 3.0 copy-start.73
  231.6 207.4 %all-reduce.17.cloned.1.call-start = ((), (), s32[]{:S(2)}) async-start(), calls=%async_computation.1 | async-start | bytes 8388608 | tf_op jit(solution)/shard_map/psum | solution.py:207
  333.1 4.0 copy-start.57
  353.2 173.2 %all-gather.8.cloned.1.call-start = ((), (), s32[]{:S(2)}) async-start(), calls=%async_computation.4 | async-start | bytes 2359296 | tf_op jit(solution)/shard_map/all_gather | solution.py:23
  439.0 5.3 copy-start.5
  439.0 6.0 copy-start.10
  439.0 6.0 copy-start.55
  439.0 6.0 copy-start.58
  444.9 3.2 copy-start.20
  444.9 3.2 copy-start.39
  444.9 3.2 copy-start.45
  444.9 3.2 copy-start.67
  445.0 3.2 copy-start.74
  455.5 410.7 %all-reduce.23.cloned.1.call-start = ((), (), s32[]{:S(2)}) async-start(), calls=%async_computation.6 | async-start | bytes 16777216 | tf_op jit(solution)/shard_map/psum | solution.py:197
  516.7 5.3 copy-start.14
  692.4 6.2 copy-start.61
  692.5 6.2 copy-start.62
  692.5 6.2 copy-start.63
  692.5 6.2 copy-start.64
  699.8 5.8 collective-permute-start.1
  714.8 274.4 %all-reduce.19.cloned.1.call-start = ((), (), s32[]{:S(2)}) async-start(), calls=%async_computation.2 | async-start | bytes 131072 | tf_op jit(solution)/shard_map/psum | solution.py:270
  715.0 5.9 copy-start.32
  715.1 5.8 copy-start.79
  720.9 3.3 copy-start.28
  720.9 3.3 copy-start.80
  724.2 3.2 copy-start.35
  733.4 676.7 %all-reduce.21.cloned.1.call-start = ((), (), s32[]{:S(2)}) async-start(), calls=%async_computation.5 | async-start | bytes 25690112 | tf_op jit(solution)/shard_map/psum | solution.py:285
  738.3 39.4 %copy-start.18 = (f32[1024,128]{1,0:T(8,128)S(1)}, f32[1024,128]{1,0:T(8,128)}, u32[]{:S(2)}) copy-start(f32[1024,128]{1,0:T(8,128)} %copy-done.17) | copy-start | bytes 1572868
  738.3 39.4 %copy-start.50 = (f32[1024,16]{0,1:T(8,128)S(1)}, f32[1024,16]{0,1:T(8,128)}, u32[]{:S(2)}) copy-start(f32[1024,16]{0,1:T(8,128)} %copy-done.49) | copy-start | bytes 196612
  738.3 127.8 %copy-start.53 = (f32[1,4,2,128]{3,1,2,0:T(4,128)S(1)}, f32[1,4,2,128]{3,1,2,0:T(4,128)}, u32[]{:S(2)}) copy-start(f32[1,4,2,128]{3,1,2,0:T(4,128)} %copy-done.52) | copy-start | bytes 12292
  738.3 127.8 %copy-start.60 = (f32[1024]{0:T(1024)S(1)}, f32[1024]{0:T(1024)}, u32[]{:S(2)}) copy-start(f32[1024]{0:T(1024)} %param.30) | copy-start | bytes 12292
  866.1 4.6 copy-start.65
  909.5 7.7 copy-start.3
  909.5 7.7 copy-start.8
  909.5 8.7 copy-start.11
  1410.1 3.9 copy-start.38
  1410.1 4.9 copy-start.37
  1420.4 4.4 copy-start.1
  (50 other events, 98.5 us)
Sparse Core Ops, SparseCore 0:
  172.7 49.7 all-gather.5
  231.7 101.3 all-reduce.14
  353.3 85.6 all-reduce.16
  455.6 49.4 all-gather.7
  714.9 151.1 all-reduce.22
  871.6 117.6 all-reduce.18
  996.6 413.4 all-reduce.20
where the time goes:
time: 1450 us; the launch traced here: 1430 us
  waiting for transfers between devices  783 us (54%)
  other arithmetic  225 us (16%)
  matrix products  157 us (11%)
  local copies, waits for them, and re-layouts  146 us (10%)
  blocking collectives  96.3 us (7%)
  between operations  15.4 us (1%)
    psum x1, waiting for transfers between devices, shards(): lax.psum((attn_gain_grad, query_weight_grad, key_weight_grad, value_weigh...  421 us
    psum x1, waiting for transfers between devices, shards(): mixer_out = lax.psum(half_dot(gated_rows, out_weight), 'head')  97.6 us
    psum x1, waiting for transfers between devices, shards(): ffn_out = lax.psum(half_dot(inner_rows, ffn_down), 'head')  88 us
    psum x1, waiting for transfers between devices, shards(): lax.psum(half_back(grad_gate, ffn_gate) + half_back(grad_up, ffn_up), 'he...  85.3 us
    dot_general x24, other arithmetic, group_step(): jnp.einsum('btd,bsd,btsd->bts', queries, key_rows, factors, precision=HIGH)  78.3 us
    psum x1, waiting for transfers between devices, shards(): lax.psum((decay_down_part, head_gain_part), ('seq', 'head'))  68.1 us
    squeeze x56, local copies, waits for them, and re-layouts, group_scan(): lax.scan(jax.checkpoint(group_step), state, (split(queries), split(key_ro...  60.5 us
    dot_general x32, matrix products, group_step(): jnp.einsum('bsk,bsv->bkv', key_rows * jnp.exp(last_row[:, None, :] - inne...  46.4 us
  transfers between devices with their start and end apart: 9, of which 7 were waited for; matrix products, arithmetic and copies ran while one was open for 9% of the time, Pallas kernels for 0%

commit v1 on v0

--- a/solution.py
+++ b/solution.py
@@ -1,10 +1,10 @@
 import jax
 import jax.numpy as jnp
+import numpy as np
 from jax import lax
+from jax.experimental import pallas as pl
+from jax.experimental.pallas import tpu as pltpu
 from jax.sharding import PartitionSpec as P
-
-GROUP = 64
-
 
 EPS = 1e-06
 HIGH = lax.Precision.HIGHEST
@@ -16,104 +16,301 @@
     return lax.ppermute(value, axis, [(source, source + steps) for source in range(initial, last)])
 
 
-def carried_in(part, axis, combine, identity, reverse):
+def rms_scale(values):
+    return lax.rsqrt(jnp.mean(values * values, axis=-1, keepdims=True) + EPS)
+
+
+def rms_back(grad_normed, normed, scale):
+    return scale * (grad_normed - normed * jnp.mean(grad_normed * normed, axis=-1, keepdims=True))
+
+
+def silu_slope(values):
+    sigma = jax.nn.sigmoid(values)
+    return sigma * (1.0 + values * (1.0 - sigma))
+
+
+def half_dot(left, right):
+    return jnp.dot(left, right, preferred_element_type=jnp.float32)
+
+
+def half_outer(left, right):
+    return lax.dot_general(
+        left, right, (((0,), (0,)), ((), ())), preferred_element_type=jnp.float32
+    )
+
+
+def half_back(left, right):
+    return lax.dot_general(
+        left, right, (((1,), (1,)), ((), ())), preferred_element_type=jnp.float32
+    )
+
+
+def exact_dot(left, right):
+    return jnp.dot(left, right, precision=HIGH, preferred_element_type=jnp.float32)
+
+
+def exact_outer(left, right):
+    return lax.dot_general(
+        left, right, (((0,), (0,)), ((), ())), precision=HIGH, preferred_element_type=jnp.float32
+    )
+
+
+def exact_back(left, right):
+    return lax.dot_general(
+        left, right, (((1,), (1,)), ((), ())), precision=HIGH, preferred_element_type=jnp.float32
+    )
+
+
+def dot3(left, right, dims):
+    left_high = left.astype(jnp.bfloat16)
+    right_high = right.astype(jnp.bfloat16)
+    left_low = (left - left_high.astype(jnp.float32)).astype(jnp.bfloat16)
+    right_low = (right - right_high.astype(jnp.float32)).astype(jnp.bfloat16)
+
+    def one(a, b):
+        return lax.dot_general(a, b, (dims, ((), ())), preferred_element_type=jnp.float32)
+
+    return one(left_high, right_high) + (one(left_high, right_low) + one(left_low, right_high))
+
+
+PLAIN = ((1,), (0,))
+BACK = ((1,), (1,))
+OUTER = ((0,), (0,))
+
+
+def sum_rows(zero_one, rows):
+    first = rows.astype(jnp.bfloat16)
+    rest = rows - first.astype(jnp.float32)
+    second = rest.astype(jnp.bfloat16)
+    third = (rest - second.astype(jnp.float32)).astype(jnp.bfloat16)
+
+    def one(part):
+        return jnp.dot(zero_one, part, preferred_element_type=jnp.float32)
+
+    return one(first) + (one(second) + one(third))
+
+
+def level_tables(size):
+    place = np.arange(size)
+    spans, masks = [], []
+    half = size // 2
+    while half >= 1:
+        odd = (place // half) % 2 == 1
+        edge = np.where(odd, (place // half) * half - 1, (place // half) * half + half - 1)
+        column = place[None, :]
+        forward = (column > edge[:, None]) & (column <= place[:, None])
+        backward = (column > place[:, None]) & (column <= edge[:, None])
+        spans.append(np.where(odd[:, None], forward, backward))
+        same = (place[:, None] // (2 * half)) == (place[None, :] // (2 * half))
+        masks.append(same & (odd[:, None] != odd[None, :]))
+        half //= 2
+    spans.append(place[None, :] <= place[:, None])
+    spans.append(place[None, :] > place[:, None])
+    return np.concatenate(spans).astype(np.float32), np.stack(masks).astype(np.float32)
+
+
+def gla_forward_kernel(
+    query, key, value, decay, spans, masks,
+    out, query_decayed, scores_out, factors_out, states, prefix, last_state, last_decay,
+    state, running,
+):
+    step = pl.program_id(0)
+    seqs, size, width = query.shape
+    levels = masks.shape[0]
+
+    @pl.when(step == 0)
+    def _():
+        state[...] = jnp.zeros_like(state)
+        running[...] = jnp.ones_like(running)
+
+    row = lax.broadcasted_iota(jnp.int32, (size, size), 0)
+    col = lax.broadcasted_iota(jnp.int32, (size, size), 1)
+    row_wide = lax.broadcasted_iota(jnp.int32, (size, width), 0)
+    for at in range(seqs):
+        q, k, v = query[at], key[at], value[at]
+        factors = jnp.exp(sum_rows(spans[...], decay[at]))
+        factors_out[at, 0] = factors
+        scores = jnp.where(row == col, jnp.sum(q * k, axis=1, keepdims=True), 0.0)
+        for level in range(levels):
+            half = size >> (level + 1)
+            odd = (row_wide // half) % 2 == 1
+            mixed = jnp.where(odd, q, k) * factors[level * size : (level + 1) * size]
+            pairs = dot3(mixed, mixed, BACK) * masks[level]
+            scores = scores + jnp.where(row > col, pairs, 0.0)
+        scores_out[at, 0] = scores
+        ahead = factors[levels * size : (levels + 1) * size]
+        behind = factors[(levels + 1) * size :]
+        whole = ahead[size - 1 : size]
+        before = state[at]
+        states[at, 0] = before
+        prior = running[at, 0:1]
+        prefix[at, 0] = running[at]
+        query_ahead = q * ahead
+        query_decayed[at] = query_ahead * prior
+        out[at] = dot3(scores, v, PLAIN) + dot3(query_ahead, before, BACK)
+        after = before * whole + dot3(v, k * behind, OUTER)
+        state[at] = after
+        running[at] = running[at] * whole
+        last_state[at] = after
+        last_decay[at] = running[at]
+
+
+def gla_backward_kernel(
+    query, key, value, grad, scores_in, factors_in, states, prefix, state_in, grad_last, masks, suffix,
+    grad_query, grad_key, grad_value, grad_decay,
+    grad_state,
+):
+    step = pl.program_id(0)
+    seqs, size, width = query.shape
+    levels = masks.shape[0]
+
+    @pl.when(step == 0)
+    def _():
+        grad_state[...] = grad_last[...]
+
+    row = lax.broadcasted_iota(jnp.int32, (size, size), 0)
+    col = lax.broadcasted_iota(jnp.int32, (size, size), 1)
+    row_wide = lax.broadcasted_iota(jnp.int32, (size, width), 0)
+    for at in range(seqs):
+        q, k, v, do = query[at], key[at], value[at], grad[at]
+        factors = factors_in[at, 0]
+        ahead = factors[levels * size : (levels + 1) * size]
+        behind = factors[(levels + 1) * size :]
+        whole = ahead[size - 1 : size]
+        before = states[at, 0] + state_in[at] * prefix[at, 0, 0:1]
+        after_grad = grad_state[at]
+        key_behind = k * behind
+        after = before * whole + dot3(v, key_behind, OUTER)
+        dv = dot3(scores_in[at, 0], do, OUTER) + dot3(key_behind, after_grad, BACK)
+        lower = dot3(do, v, BACK)
+        both = jnp.where(row >= col, lower, dot3(v, do, BACK))
+        diagonal = jnp.sum(do * v, axis=1, keepdims=True)
+        dq = dot3(do, before, PLAIN) * ahead
+        dk = dot3(v, after_grad, PLAIN) * behind
+        for level in range(levels):
+            half = size >> (level + 1)
+            odd = (row_wide // half) % 2 == 1
+            factor = factors[level * size : (level + 1) * size]
+            mixed = jnp.where(odd, q, k) * factor
+            back = dot3(both * masks[level], mixed, PLAIN) * factor
+            dq = dq + jnp.where(odd, back, 0.0)
+            dk = dk + jnp.where(odd, 0.0, back)
+        carried = jnp.sum(after * after_grad, axis=0, keepdims=True)
+        grad_decay[at] = sum_rows(suffix[...], q * dq - k * dk) + carried
+        grad_query[at] = dq + diagonal * k
+        grad_key[at] = dk + diagonal * q
+        grad_value[at] = dv
+        grad_state[at] = after_grad * whole + dot3(do, q * ahead, OUTER)
+
+
+def chunk_of(count):
+    size = 128
+    while count % size:
+        size //= 2
+    return size
+
+
+def gla_forward(query, key, value, decay):
+    seqs, count, width = query.shape
+    values = value.shape[2]
+    size = chunk_of(count)
+    chunks = count // size
+    spans, masks = level_tables(size)
+    tall = spans.shape[0]
+
+    def rows(columns):
+        return pl.BlockSpec((seqs, size, columns), lambda i: (0, i, 0))
+
+    def whole(*shape):
+        return pl.BlockSpec(shape, lambda i: (0,) * len(shape))
+
+    def chunk(*shape):
+        return pl.BlockSpec((seqs, 1) + shape, lambda i: (0, i, 0, 0))
+
+    f32 = jnp.float32
+    return pl.pallas_call(
+        gla_forward_kernel,
+        grid=(chunks,),
+        in_specs=[rows(width), rows(width), rows(values), rows(width), whole(*spans.shape), whole(*masks.shape)],
+        out_specs=[
+            rows(values), rows(width), chunk(size, size), chunk(tall, width),
+            chunk(values, width), chunk(8, width), whole(seqs, values, width), whole(seqs, 8, width),
+        ],
+        out_shape=[
+            jax.ShapeDtypeStruct((seqs, count, values), f32),
+            jax.ShapeDtypeStruct((seqs, count, width), f32),
+            jax.ShapeDtypeStruct((seqs, chunks, size, size), f32),
+            jax.ShapeDtypeStruct((seqs, chunks, tall, width), f32),
+            jax.ShapeDtypeStruct((seqs, chunks, values, width), f32),
+            jax.ShapeDtypeStruct((seqs, chunks, 8, width), f32),
+            jax.ShapeDtypeStruct((seqs, values, width), f32),
+            jax.ShapeDtypeStruct((seqs, 8, width), f32),
+        ],
+        scratch_shapes=[pltpu.VMEM((seqs, values, width), f32), pltpu.VMEM((seqs, 8, width), f32)],
+        compiler_params=pltpu.CompilerParams(vmem_limit_bytes=48 * 1024 * 1024),
+        name="gla_local",
+    )(query, key, value, decay, jnp.asarray(spans, jnp.bfloat16), jnp.asarray(masks))
+
+
+def gla_backward(query, key, value, grad, scores, factors, states, prefix, state_in, grad_last):
+    seqs, count, width = query.shape
+    values = value.shape[2]
+    size = chunk_of(count)
+    chunks = count // size
+    spans, masks = level_tables(size)
+    tall = spans.shape[0]
+    suffix = np.triu(np.ones((size, size), np.float32))
+
+    def rows(columns):
+        return pl.BlockSpec((seqs, size, columns), lambda i: (0, chunks - 1 - i, 0))
+
+    def whole(*shape):
+        return pl.BlockSpec(shape, lambda i: (0,) * len(shape))
+
+    def chunk(*shape):
+        return pl.BlockSpec((seqs, 1) + shape, lambda i: (0, chunks - 1 - i, 0, 0))
+
+    f32 = jnp.float32
+    return pl.pallas_call(
+        gla_backward_kernel,
+        grid=(chunks,),
+        in_specs=[
+            rows(width), rows(width), rows(values), rows(values), chunk(size, size), chunk(tall, width),
+            chunk(values, width), chunk(8, width), whole(seqs, values, width), whole(seqs, values, width),
+            whole(*masks.shape), whole(*suffix.shape),
+        ],
+        out_specs=[rows(width), rows(width), rows(values), rows(width)],
+        out_shape=[
+            jax.ShapeDtypeStruct((seqs, count, width), f32),
+            jax.ShapeDtypeStruct((seqs, count, width), f32),
+            jax.ShapeDtypeStruct((seqs, count, values), f32),
+            jax.ShapeDtypeStruct((seqs, count, width), f32),
+        ],
+        scratch_shapes=[pltpu.VMEM((seqs, values, width), f32)],
+        compiler_params=pltpu.CompilerParams(vmem_limit_bytes=48 * 1024 * 1024),
+        name="gla_back",
+    )(query, key, value, grad, scores, factors, states, prefix, state_in, grad_last,
+      jnp.asarray(masks), jnp.asarray(suffix, jnp.bfloat16))
+
+
+def carried_in(decay, state, axis, reverse):
     count = lax.axis_size(axis)
     place = lax.axis_index(axis)
     ahead = count - 1 - place if reverse else place
-    gathered = jax.tree.map(lambda a: lax.all_gather(a, axis), part)
-    state = jax.tree.map(lambda a, e: jnp.zeros_like(a) + jnp.asarray(e, a.dtype), part, identity)
-
-    def one(turn, state):
+    values = state.shape[1]
+    gathered = lax.all_gather(jnp.concatenate([state, decay], axis=1), axis)
+    total = jnp.zeros_like(state)
+
+    def one(turn, total):
         source = count - 1 - turn if reverse else turn
-        return combine(
-            state, jax.tree.map(lambda a: lax.dynamic_index_in_dim(a, source, 0, False), gathered)
-        )
-
-    return lax.fori_loop(0, ahead, one, state)
-
-
-def rms_scale(values):
-    return lax.rsqrt(jnp.mean(values * values, axis=-1, keepdims=True) + EPS)
-
-
-def rms_back(grad_normed, normed, scale):
-    return scale * (grad_normed - normed * jnp.mean(grad_normed * normed, axis=-1, keepdims=True))
-
-
-def silu_slope(values):
-    sigma = jax.nn.sigmoid(values)
-    return sigma * (1.0 + values * (1.0 - sigma))
-
-
-def half_dot(left, right):
-    return jnp.dot(left, right, preferred_element_type=jnp.float32)
-
-
-def half_outer(left, right):
-    return lax.dot_general(
-        left, right, (((0,), (0,)), ((), ())), preferred_element_type=jnp.float32
-    )
-
-
-def half_back(left, right):
-    return lax.dot_general(
-        left, right, (((1,), (1,)), ((), ())), preferred_element_type=jnp.float32
-    )
-
-
-def exact_dot(left, right):
-    return jnp.dot(left, right, precision=HIGH, preferred_element_type=jnp.float32)
-
-
-def exact_outer(left, right):
-    return lax.dot_general(
-        left, right, (((0,), (0,)), ((), ())), precision=HIGH, preferred_element_type=jnp.float32
-    )
-
-
-def exact_back(left, right):
-    return lax.dot_general(
-        left, right, (((1,), (1,)), ((), ())), precision=HIGH, preferred_element_type=jnp.float32
-    )
-
-
-def group_step(state, pieces):
-    queries, key_rows, value_rows, decay_log = pieces
-    inner = jnp.cumsum(decay_log, axis=1)
-    count = inner.shape[1]
-    lower = (jnp.arange(count)[:, None] >= jnp.arange(count)[None, :])[None, :, :, None]
-    spread = inner[:, :, None, :] - inner[:, None, :, :]
-    factors = jnp.exp(jnp.where(lower, spread, 0.0)) * lower.astype(jnp.float32)
-    scores = jnp.einsum("btd,bsd,btsd->bts", queries, key_rows, factors, precision=HIGH)
-    output = jnp.einsum("bts,bsv->btv", scores, value_rows, precision=HIGH)
-    output = output + jnp.einsum("btk,bkv->btv", queries * jnp.exp(inner), state, precision=HIGH)
-    last_row = inner[:, -1, :]
-    carried = jnp.einsum(
-        "bsk,bsv->bkv", key_rows * jnp.exp(last_row[:, None, :] - inner), value_rows, precision=HIGH
-    )
-    state = jnp.exp(last_row)[:, :, None] * state + carried
-    return (state, output)
-
-
-def group_scan(queries, key_rows, value_rows, decay_log, state, group_len):
-    count = queries.shape[1]
-
-    def split(values):
-        return jnp.moveaxis(
-            values.reshape(values.shape[0], count // group_len, group_len, values.shape[2]), 1, 0
-        )
-
-    state, output = lax.scan(
-        jax.checkpoint(group_step),
-        state,
-        (split(queries), split(key_rows), split(value_rows), split(decay_log)),
-    )
-    output = jnp.moveaxis(output, 0, 1).reshape(queries.shape[0], count, value_rows.shape[2])
-    return (output, state)
-
-
-def link_states(earlier, later):
-    return (earlier[0] * later[0], later[0][:, :, None] * earlier[1] + later[1])
+        part = lax.dynamic_index_in_dim(gathered, source, 0, False)
+        return jnp.where(turn < ahead, total * part[:, values : values + 1] + part[:, :values], total)
+
+    if count <= 16:
+        for turn in range(count - 1):
+            total = one(turn, total)
+        return total
+    return lax.fori_loop(0, count - 1, one, total)
 
 
 def shards(
@@ -170,16 +367,11 @@
     queries = conv_out[:, :, :key_size] * factor
     key_rows = conv_out[:, :, key_size : 2 * key_size]
     value_rows = conv_out[:, :, 2 * key_size :]
-    zero_state = jnp.zeros((seq_count, key_size, value_size), jnp.float32)
-    local_out, local_state = group_scan(queries, key_rows, value_rows, decay_log, zero_state, GROUP)
-    running = jnp.cumsum(decay_log, axis=1)
-    query_decayed = queries * jnp.exp(running)
-    block_decay = jnp.exp(running[:, -1])
-    unit_decay = jnp.ones_like(block_decay)
-    prior, state_in = carried_in(
-        (block_decay, local_state), "seq", link_states, (unit_decay, zero_state), False
-    )
-    mixed_rows = local_out + jnp.einsum("btk,bkv->btv", query_decayed, state_in, precision=HIGH)
+    local_out, query_decayed, scores, factors, states, prefix, local_state, block_decay = gla_forward(
+        queries, key_rows, value_rows, decay_log
+    )
+    state_in = carried_in(block_decay, local_state, "seq", False)
+    mixed_rows = local_out + jnp.einsum("btk,bvk->btv", query_decayed, state_in, precision=HIGH)
     mixed_rows = mixed_rows.reshape(row_count, value_size)
     head_scale = rms_scale(mixed_rows)
     head_normed = mixed_rows * head_scale
@@ -216,16 +408,11 @@
     grad_mixed = rms_back(grad_normed * head_gain, head_normed, head_scale).reshape(
         seq_count, tok_rows, value_size
     )
-    state_pull = jnp.einsum("btk,btv->bkv", query_decayed, grad_mixed, precision=HIGH)
-    later, grad_state_out = carried_in(
-        (block_decay, state_pull), "seq", link_states, (unit_decay, zero_state), True
-    )
-
-    def attend(query_part, key_part, value_part, decay_part):
-        return group_scan(query_part, key_part, value_part, decay_part, state_in, GROUP)
-
-    unused, attend_back = jax.vjp(attend, queries, key_rows, value_rows, decay_log)
-    grad_queries, grad_keys, grad_values, grad_decay = attend_back((grad_mixed, grad_state_out))
+    state_pull = jnp.einsum("btk,btv->bvk", query_decayed, grad_mixed, precision=HIGH)
+    grad_state_out = carried_in(block_decay, state_pull, "seq", True)
+    grad_queries, grad_keys, grad_values, grad_decay = gla_backward(
+        queries, key_rows, value_rows, grad_mixed, scores, factors, states, prefix, state_in, grad_state_out
+    )
     grad_conv_out = jnp.concatenate([grad_queries * factor, grad_keys, grad_values], axis=2)
     grad_conv_pre = grad_conv_out * silu_slope(conv_pre)
     grad_padded = jnp.zeros_like(padded)

time: 1450 us -> 1120 us (0.77)
  other arithmetic: 225 us -> 50.7 us
  local copies, waits for them, and re-layouts: 146 us -> 38.2 us
  matrix products: 157 us -> 64.4 us
  waiting for transfers between devices: 783 us -> 837 us
  Pallas kernels: 0 us -> 23.4 us
  blocking collectives: 96.3 us -> 79.3 us
    dot_general x82 -> x2, matrix products: 94.4 us -> 2.87 us  [the longest x1 1.88 us: shards(): jnp.einsum('btk,btv->bvk', query_decayed, grad_mixed, precision=HIGH)]
    dot_general x24 -> x0, other arithmetic: 78.3 us -> none  [group_step(): jnp.einsum('btd,bsd,btsd->bts', queries, key_rows, factors, precision=HIGH)]
    all_gather x2, waiting for transfers between devices: 20.4 us -> 92.4 us  [carried_in(): gathered = lax.all_gather(jnp.concatenate([state, decay], axis=1), axis)]
    squeeze x56 -> x0, local copies, waits for them, and re-layouts: 60.5 us -> none  [group_scan(): lax.scan(jax.checkpoint(group_step), state, (split(queries), split(key_ro...]
    reduce_sum x24 -> x0, other arithmetic: 35.3 us -> none  [the longest x8 34.1 us: group_step(): spread = inner[:, :, None, :] - inner[:, None, :, :]]
    another operation x44 -> x2, other arithmetic: 34.4 us -> 1.69 us  [one(): total * part[:, values:values + 1] + part[:, :values]]
    pallas_call x0 -> x2, Pallas kernels: none -> 23.4 us  [the longest x1 13.5 us: gla_forward(): pl.pallas_call(gla_forward_kernel, grid=(chunks,), in_specs=[rows(width),...]
    all_gather x1 -> x0, blocking collectives: 19.5 us -> none  [carried_in(): gathered = jax.tree.map(lambda a: lax.all_gather(a, axis), part)]
  transfers between devices with their start and end apart: 9 -> 9, of which waited for: 7 -> 8; matrix products, arithmetic and copies ran while one was open for 9% -> 5% of each run, Pallas kernels for 0% -> 0%
where the time goes in v1:
time: 1120 us
  waiting for transfers between devices  837 us (75%)
  blocking collectives  79.3 us (7%)
  matrix products  64.4 us (6%)
  other arithmetic  50.7 us (5%)
  local copies, waits for them, and re-layouts  38.2 us (3%)
  Pallas kernels  23.4 us (2%)
  between operations  15.4 us (1%)
    psum x1, waiting for transfers between devices, shards(): lax.psum((attn_gain_grad, query_weight_grad, key_weight_grad, value_weigh...  421 us
    all_gather x2, waiting for transfers between devices, carried_in(): gathered = lax.all_gather(jnp.concatenate([state, decay], axis=1), axis)  92.4 us
    psum x1, waiting for transfers between devices, shards(): ffn_out = lax.psum(half_dot(inner_rows, ffn_down), 'head')  87.6 us
    psum x1, waiting for transfers between devices, shards(): lax.psum(half_back(grad_gate, ffn_gate) + half_back(grad_up, ffn_up), 'he...  85.6 us
    psum x1, waiting for transfers between devices, shards(): mixer_out = lax.psum(half_dot(gated_rows, out_weight), 'head')  79.7 us
    psum x1, waiting for transfers between devices, shards(): lax.psum((decay_down_part, head_gain_part), ('seq', 'head'))  68.6 us
    psum x1, blocking collectives, shards(): lax.psum((decay_down_part, head_gain_part), ('seq', 'head'))  41.6 us
    psum x1, blocking collectives, shards(): lax.psum((attn_gain_grad, query_weight_grad, key_weight_grad, value_weigh...  37.7 us
  transfers between devices with their start and end apart: 9, of which 8 were waited for; matrix products, arithmetic and copies ran while one was open for 5% of the time, Pallas kernels for 0%

profile of v1, /device:TPU:0, one launch (start us, length us, event | category | flops | bytes accessed | tf_op | source)
XLA Modules:
  0.0 1116.4 jit_solution(6615270593418920196)
XLA Ops:
  7.3 2.7 multiply_reduce_fusion.5
  16.2 2.9 copy.44
  20.0 4.9 collective-permute-start
  28.6 2.2 fusion.4
  32.0 13.5 %gla_local.1 = (f32[2,512,256]{2,1,0:T(8,128)S(1)}, f32[2,512,128]{2,1,0:T(8,128)S(1)}, f32[2,4,128,128]{3,2,1,0:T(8,128)S(1)}, f32[2,4,1152,128]{3,2,1,0:T(8,12...) custom-call(f32[2,512,128]{2,1,0:T(8,128)S(1)} %get-tuple-element.10, ...), custom_call_target="tpu_custom_call" | custom-call | tf_op jit(solution)/shard_map/gla_local/pallas_call | solution.py:231
  49.0 50.3 %all-gather.5.cloned.1.call-done = f32[16,264,128]{2,1,0:T(8,128)} async-done(((f32[2,264,128]{2,1,0:T(8,128)}), f32[16,264,128]{2,1,0:T(8,128)}) %all-gather.5.cloned.1.call-update) | async-done | bytes 2162704 | tf_op jit(solution)/shard_map/all_gather | solution.py:301
  100.3 1.6 fusion.23.state_in
  103.6 1.8 multiply_convert_fusion.6
  106.1 2.7 fusion.48
  109.4 3.9 bitcast_convert_fusion
  113.3 79.7 %all-reduce.14.cloned.1.call-done = f32[1024,1024]{1,0:T(8,128)} async-done(((f32[1024,1024]{1,0:T(8,128)}), f32[1024,1024]{1,0:T(8,128)}) %all-reduce.14.cloned.1.call-update) | async-done | bytes 4194320 | tf_op jit(solution)/shard_map/psum | solution.py:381
  193.0 4.0 multiply_reduce_fusion.4
  199.5 1.7 fusion.49
  201.6 1.7 fusion.50
  203.3 3.9 multiply_convert_fusion.2
  207.2 1.8 fusion.52
  209.1 3.9 convolution_add_fusion
  213.3 85.6 %all-reduce.16.cloned.1.call-done = f32[1024,1024]{1,0:T(8,128)} async-done(((f32[1024,1024]{1,0:T(8,128)}), f32[1024,1024]{1,0:T(8,128)}) %all-reduce.16.cloned.1.call-update) | async-done | bytes 4194320 | tf_op jit(solution)/shard_map/psum | solution.py:399
  298.9 5.3 multiply_reduce_fusion
  304.8 3.1 bitcast_add_fusion
  308.0 1.9 multiply_reduce_fusion.10
  311.5 1.9 fusion.53
  314.2 5.3 fusion.51
  319.5 2.8 fusion.54
  322.4 42.0 %all-gather.7.cloned.1.call-done = f32[16,264,128]{2,1,0:T(8,128)} async-done(((f32[2,264,128]{2,1,0:T(8,128)}), f32[16,264,128]{2,1,0:T(8,128)}) %all-gather.7.cloned.1.call-update) | async-done | bytes 2162704 | tf_op jit(solution)/shard_map/all_gather | solution.py:301
  365.2 1.6 fusion.16.grad_last
  366.9 9.9 gla_back.1
  378.4 1.7 multiply_reduce_fusion.9
  381.2 1.6 collective-permute-start.1
  384.5 2.5 collective-permute-done.1
  391.4 4.8 add_add_fusion
  397.8 4.7 fusion.60
  402.5 3.3 fusion.61
  405.7 3.2 fusion.59
  409.0 1.7 fusion.56
  411.7 1.7 fusion.5
  415.3 1.7 fusion.12
  420.8 41.6 %psum.146 = f32[256]{0:T(256)} all-reduce(f32[256]{0:T(256)S(1)} %copy-done.72), channel_id=1, replica_groups=mesh['seq'=8,'head'=4] {'seq','head'}, use_global_device_ids=true, to_apply=%region_26.27 | all-reduce | flops 256 | bytes 2048 | tf_op jit(solution)/shard_map/psum | solution.py:457
  462.8 87.6 %all-reduce.22.cloned.1.call-done = (f32[1024,1024]{1,0:T(8,128)}, f32[1024,1024]{1,0:T(8,128)}) async-done(((f32[1024,1024]{1,0:T(8,128)}, f32[1024,1024]{1,0:T(8,128)}), (f32[1024,1024]{1,0:T(8,128)}, f32[1024,1024]{1,0:T(8,128)})) %all-reduce.22.cloned.1.call-update) | async-done | bytes 8388624 | tf_op jit(solution)/shard_map/psum | solution.py:389
  550.4 4.6 multiply_reduce_fusion.1
  554.9 37.7 %all-reduce.5 = (f32[1024]{0:T(1024)}, f32[16,128]{1,0:T(8,128)}, f32[128]{0:T(128)}, f32[4,512]{1,0:T(4,128)S(1)}, f32[1024]{0:T(1024)}) all-reduce(f32[1024]{0:T(1024)S(1)} %get-tuple-element.45, f32[16,128]{1,0:T(8,128)S(1)} %fusion.58, f32[128]{0:T(128)S(1)} %get-tuple-element.69, ...), channel_id=1, replica_groups=mesh['seq'=8,'head'=4] {'seq'}, use_global_device_ids=true, to_apply=%region_11.12 | all-reduce | flops 6272 | bytes 50176 | tf_op jit(solution)/shard_map/psum | solution.py:472
  593.3 7.1 add.244
  601.9 2.9 multiply_add_fusion
  604.9 68.6 %all-reduce.18.cloned.1.call-done = f32[1024,16]{0,1:T(8,128)} async-done(((f32[1024,16]{0,1:T(8,128)}), f32[1024,16]{0,1:T(8,128)}) %all-reduce.18.cloned.1.call-update) | async-done | bytes 65552 | tf_op jit(solution)/shard_map/psum | solution.py:457
  673.5 420.9 %all-reduce.20.cloned.1.call-done = (f32[1024,128]{1,0:T(8,128)}, f32[1024,128]{1,0:T(8,128)}, f32[1024,256]{1,0:T(8,128)}, f32[1024,256]{1,0:T(8,128)}, f32[256...) async-done(((f32[1024,128]{1,0:T(8,128)}, f32[1024,128]{1,0:T(8,128)}, f32[1024,256]{1,0:T(8,128)}, f32[1024,256]{1,0:T(8,128)}, ...) | async-done | bytes 12845072 | tf_op jit(solution)/shard_map/psum | solution.py:472
  1094.3 2.0 copy.64
  1096.3 1.9 copy.65
  1101.8 1.6 copy.70
  (230 shorter events, 55.0 us)
Async XLA Ops:
  7.2 196.1 %copy-start = (bf16[704,1024]{1,0:T(8,128)(2,1)S(1)}, bf16[704,1024]{1,0:T(8,128)(2,1)}, u32[]{:S(2)}) copy-start(bf16[704,1024]{1,0:T(8,128)(2,1)} %param.40) | copy-start | bytes 4325380
  7.2 92.2 %all-gather.5.cloned.1.call-start = ((), (), s32[]{:S(2)}) async-start(), calls=%async_computation.3 | async-start | bytes 2433024 | tf_op jit(solution)/shard_map/all_gather | solution.py:301
  7.3 3.5 copy-start.14
  11.8 13.7 %copy-start.11 = (bf16[1024,1024]{1,0:T(8,128)(2,1)}, bf16[1024,1024]{1,0:T(8,128)(2,1)S(1)}, u32[]{:S(2)}) copy-start(bf16[1024,1024]{1,0:T(8,128)(2,1)S(1)} %multiply_convert_fusion.1) | copy-start | bytes 6291460
  19.1 7.9 copy-start.71
  19.1 7.9 copy-start.70
  19.1 7.9 copy-start.68
  19.1 8.0 copy-start.76
  19.1 9.5 copy-start.21
  20.0 8.6 collective-permute-start
  49.0 144.1 %all-reduce.14.cloned.1.call-start = ((), (), s32[]{:S(2)}) async-start(), calls=%async_computation | async-start | bytes 8388608 | tf_op jit(solution)/shard_map/psum | solution.py:381
  99.4 3.5 copy-start.6
  108.9 190.0 %all-reduce.16.cloned.1.call-start = ((), (), s32[]{:S(2)}) async-start(), calls=%async_computation.1 | async-start | bytes 8388608 | tf_op jit(solution)/shard_map/psum | solution.py:399
  113.3 83.8 %copy-start.64 = (f32[1024]{0:T(1024)S(1)}, f32[1024]{0:T(1024)}, u32[]{:S(2)}) copy-start(f32[1024]{0:T(1024)} %param.37) | copy-start | bytes 12292
  213.1 151.3 %all-gather.7.cloned.1.call-start = ((), (), s32[]{:S(2)}) async-start(), calls=%async_computation.4 | async-start | bytes 2433024 | tf_op jit(solution)/shard_map/all_gather | solution.py:301
  298.9 5.3 copy-start.17
  298.9 5.9 copy-start.24
  304.8 3.2 copy-start.31
  304.8 3.2 copy-start.48
  304.8 3.2 copy-start.54
  314.1 236.2 %all-reduce.22.cloned.1.call-start = ((), (), s32[]{:S(2)}) async-start(), calls=%async_computation.6 | async-start | bytes 16777216 | tf_op jit(solution)/shard_map/psum | solution.py:389
  314.2 5.3 copy-start.43
  314.2 5.3 copy-start.56
  322.4 44.5 %copy-start.3 = (f32[7,128,128]{2,1,0:T(8,128)S(1)}, f32[7,128,128]{2,1,0:T(8,128)}, u32[]{:S(2)}) copy-start(f32[7,128,128]{2,1,0:T(8,128)} %constant.104.clone.masks) | copy-start | bytes 1376260
  322.4 44.5 %copy-start.8 = (f32[2,4,128,128]{3,2,1,0:T(8,128)S(1)}, f32[2,4,128,128]{3,2,1,0:T(8,128)}, u32[]{:S(2)}) copy-start(f32[2,4,128,128]{3,2,1,0:T(8,128)} %copy-done.7) | copy-start | bytes 1572868
  322.4 44.5 %copy-start.10 = (bf16[128,128]{1,0:T(8,128)(2,1)S(1)}, bf16[128,128]{1,0:T(8,128)(2,1)}, u32[]{:S(2)}) copy-start(bf16[128,128]{1,0:T(8,128)(2,1)} %constant.105.clone.suffix) | copy-start | bytes 98308
  366.9 10.1 copy-start.27
  381.2 5.8 collective-permute-start.1
  396.2 277.3 %all-reduce.18.cloned.1.call-start = ((), (), s32[]{:S(2)}) async-start(), calls=%async_computation.2 | async-start | bytes 131072 | tf_op jit(solution)/shard_map/psum | solution.py:457
  397.8 4.7 copy-start.78
  402.5 3.3 copy-start.38
  402.5 3.3 copy-start.79
  405.7 3.3 copy-start.13
  405.7 3.3 copy-start.44
  415.0 679.4 %all-reduce.20.cloned.1.call-start = ((), (), s32[]{:S(2)}) async-start(), calls=%async_computation.5 | async-start | bytes 25690112 | tf_op jit(solution)/shard_map/psum | solution.py:472
  420.1 42.3 %copy-start.29 = (f32[1024,128]{1,0:T(8,128)S(1)}, f32[1024,128]{1,0:T(8,128)}, u32[]{:S(2)}) copy-start(f32[1024,128]{1,0:T(8,128)} %copy-done.28) | copy-start | bytes 1572868
  420.1 42.3 %copy-start.59 = (f32[1024,16]{0,1:T(8,128)S(1)}, f32[1024,16]{0,1:T(8,128)}, u32[]{:S(2)}) copy-start(f32[1024,16]{0,1:T(8,128)} %copy-done.58) | copy-start | bytes 196612
  420.1 130.2 %copy-start.62 = (f32[1,4,2,128]{3,1,2,0:T(4,128)S(1)}, f32[1,4,2,128]{3,1,2,0:T(4,128)}, u32[]{:S(2)}) copy-start(f32[1,4,2,128]{3,1,2,0:T(4,128)} %copy-done.61) | copy-start | bytes 12292
  420.1 130.2 %copy-start.66 = (f32[1024]{0:T(1024)S(1)}, f32[1024]{0:T(1024)}, u32[]{:S(2)}) copy-start(f32[1024]{0:T(1024)} %param.24) | copy-start | bytes 12292
  550.4 4.6 copy-start.67
  593.3 7.7 copy-start.15
  593.3 7.7 copy-start.20
  593.3 8.7 copy-start.25
  1094.3 3.9 copy-start.47
  1094.3 4.9 copy-start.46
  1101.8 2.9 copy-start.35
  1104.6 2.9 copy-start.34
  1104.6 4.4 copy-start.1
  (42 other events, 72.2 us)
Sparse Core Ops, SparseCore 0:
  49.1 50.2 all-gather.4
  109.0 83.9 all-reduce.13
  213.2 85.6 all-reduce.15
  314.3 50.0 all-gather.6
  396.3 154.0 all-reduce.21
  555.8 117.6 all-reduce.17
  680.8 413.4 all-reduce.19

commit v2 on v1

--- a/solution.py
+++ b/solution.py
@@ -1,3 +1,5 @@
+import functools
+
 import jax
 import jax.numpy as jnp
 import numpy as np
@@ -293,24 +295,151 @@
       jnp.asarray(masks), jnp.asarray(suffix, jnp.bfloat16))
 
 
-def carried_in(decay, state, axis, reverse):
+MESH = pl.DeviceIdType.MESH
+
+
+def greet(axis, partners):
+    barrier = pltpu.get_barrier_semaphore()
+    for partner in partners:
+        pl.semaphore_signal(barrier, inc=1, device_id={axis: partner}, device_id_type=MESH)
+    pl.semaphore_wait(barrier, len(partners))
+
+
+def prefix_kernel(axis, reverse, block, out, total, received, send_sem, recv_sem):
+    steps, seqs, tall, width = total.shape
+    values = tall - 8
+    me = lax.axis_index(axis)
+    uppers = [(me // (1 << step)) % 2 for step in range(steps)]
+    partners = [me + (1 << step) * (1 - 2 * upper) for step, upper in enumerate(uppers)]
+    greet(axis, partners)
+    total[0] = block[...]
+    out[...] = jnp.zeros_like(out)
+    passed = jnp.ones((seqs, 1, width), jnp.float32)
+    for step in range(steps):
+        copy = pltpu.make_async_remote_copy(
+            src_ref=total.at[step],
+            dst_ref=received.at[step],
+            send_sem=send_sem.at[step],
+            recv_sem=recv_sem.at[step],
+            device_id={axis: partners[step]},
+            device_id_type=MESH,
+        )
+        copy.start()
+        copy.wait()
+        later = uppers[step] == (0 if reverse else 1)
+        theirs = received[step, :, :values]
+        their_decay = received[step, :, values:]
+        out[...] = jnp.where(later, theirs * passed + out[...], out[...])
+        passed = jnp.where(later, their_decay[:, 0:1] * passed, passed)
+        if step + 1 < steps:
+            mine = total[step, :, :values]
+            my_decay = total[step, :, values:]
+            total[step + 1, :, :values] = jnp.where(
+                later, theirs * my_decay[:, 0:1] + mine, mine * their_decay[:, 0:1] + theirs
+            )
+            total[step + 1, :, values:] = my_decay * their_decay
+
+
+def carried_in(decay, state, axis, reverse, call_id):
     count = lax.axis_size(axis)
-    place = lax.axis_index(axis)
-    ahead = count - 1 - place if reverse else place
-    values = state.shape[1]
-    gathered = lax.all_gather(jnp.concatenate([state, decay], axis=1), axis)
-    total = jnp.zeros_like(state)
-
-    def one(turn, total):
-        source = count - 1 - turn if reverse else turn
-        part = lax.dynamic_index_in_dim(gathered, source, 0, False)
-        return jnp.where(turn < ahead, total * part[:, values : values + 1] + part[:, :values], total)
-
-    if count <= 16:
-        for turn in range(count - 1):
-            total = one(turn, total)
-        return total
-    return lax.fori_loop(0, count - 1, one, total)
+    steps = count.bit_length() - 1
+    assert count == 1 << steps
+    block = jnp.concatenate([state, decay], axis=1)
+    slots = pltpu.VMEM((steps,) + block.shape, jnp.float32)
+    return pl.pallas_call(
+        functools.partial(prefix_kernel, axis, reverse),
+        out_shape=jax.ShapeDtypeStruct(state.shape, jnp.float32),
+        in_specs=[pl.BlockSpec(memory_space=pltpu.VMEM)],
+        out_specs=pl.BlockSpec(memory_space=pltpu.VMEM),
+        scratch_shapes=[slots, slots, pltpu.SemaphoreType.DMA((steps,)), pltpu.SemaphoreType.DMA((steps,))],
+        compiler_params=pltpu.CompilerParams(
+            collective_id=call_id, has_side_effects=True, vmem_limit_bytes=32 * 1024 * 1024
+        ),
+        name="state_prefix",
+    )(block)
+
+
+def sum_kernel(axis, terms, out, partial, from_near, from_far, send_sem, recv_sem):
+    pieces = terms.shape[0]
+    me = lax.axis_index(axis)
+    low, high = me % 2, me // 2
+    near = me + 1 - 2 * low
+    far = me + 2 - 4 * high
+    mine = 2 * low + high
+    other = 2 * low + 1 - high
+    greet(axis, [near, far])
+
+    def copy(kind, piece, source, target, device):
+        return pltpu.make_async_remote_copy(
+            src_ref=source,
+            dst_ref=target,
+            send_sem=send_sem.at[kind, piece],
+            recv_sem=recv_sem.at[kind, piece],
+            device_id={axis: device},
+            device_id_type=MESH,
+        )
+
+    def halves(piece):
+        return copy(0, piece, terms.at[piece, pl.ds(2 - 2 * low, 2)], from_near.at[piece], near)
+
+    def quarters(piece):
+        return copy(1, piece, partial.at[piece, 1 - high], from_far.at[piece], far)
+
+    def back_far(piece):
+        return copy(2, piece, out.at[piece, mine], out.at[piece, mine], far)
+
+    def back_near(piece):
+        return copy(3, piece, out.at[piece, mine], out.at[piece, mine], near)
+
+    def pass_near(piece):
+        return copy(4, piece, out.at[piece, other], out.at[piece, other], near)
+
+    for piece in range(pieces):
+        halves(piece).start()
+    for piece in range(pieces):
+        halves(piece).wait_recv()
+        partial[piece] = terms[piece, pl.ds(2 * low, 2)] + from_near[piece]
+        quarters(piece).start()
+    for piece in range(pieces):
+        quarters(piece).wait_recv()
+        out[piece, mine] = partial[piece, high] + from_far[piece]
+        back_far(piece).start()
+        back_near(piece).start()
+    for piece in range(pieces):
+        back_far(piece).wait_recv()
+        pass_near(piece).start()
+    for piece in range(pieces):
+        back_near(piece).wait_recv()
+        pass_near(piece).wait_recv()
+        for made in (halves, quarters, back_far, back_near, pass_near):
+            made(piece).wait_send()
+
+
+def head_sum(terms, axis, call_id):
+    rows, columns = terms.shape
+    if lax.axis_size(axis) != 4 or rows % 32:
+        return lax.psum(terms, axis)
+    pieces = next(count for count in (4, 5, 3, 2, 1) if rows % (32 * count) == 0)
+    deep = rows // (4 * pieces)
+    f32 = jnp.float32
+    out = pl.pallas_call(
+        functools.partial(sum_kernel, axis),
+        out_shape=jax.ShapeDtypeStruct((pieces, 4, deep, columns), f32),
+        in_specs=[pl.BlockSpec(memory_space=pltpu.VMEM)],
+        out_specs=pl.BlockSpec(memory_space=pltpu.VMEM),
+        scratch_shapes=[
+            pltpu.VMEM((pieces, 2, deep, columns), f32),
+            pltpu.VMEM((pieces, 2, deep, columns), f32),
+            pltpu.VMEM((pieces, deep, columns), f32),
+            pltpu.SemaphoreType.DMA((5, pieces)),
+            pltpu.SemaphoreType.DMA((5, pieces)),
+        ],
+        compiler_params=pltpu.CompilerParams(
+            collective_id=call_id, has_side_effects=True, vmem_limit_bytes=48 * 1024 * 1024
+        ),
+        name="head_sum",
+    )(terms.reshape(pieces, 4, deep, columns))
+    return out.reshape(rows, columns)
 
 
 def shards(
@@ -370,7 +499,7 @@
     local_out, query_decayed, scores, factors, states, prefix, local_state, block_decay = gla_forward(
         queries, key_rows, value_rows, decay_log
     )
-    state_in = carried_in(block_decay, local_state, "seq", False)
+    state_in = carried_in(block_decay, local_state, "seq", False, 0)
     mixed_rows = local_out + jnp.einsum("btk,bvk->btv", query_decayed, state_in, precision=HIGH)
     mixed_rows = mixed_rows.reshape(row_count, value_size)
     head_scale = rms_scale(mixed_rows)
@@ -378,7 +507,7 @@
     normed_gain = head_normed * head_gain
     gate_act = jax.nn.silu(gate_raw)
     gated_rows = (normed_gain * gate_act).astype(jnp.bfloat16)
-    mixer_out = lax.psum(half_dot(gated_rows, out_weight), "head")
+    mixer_out = head_sum(half_dot(gated_rows, out_weight), "head", 2)
     middle = inputs + mixer_out
     scale_two = rms_scale(middle)
     normed_two = middle * scale_two
@@ -386,8 +515,7 @@
     gate_rows = half_dot(hidden_two, ffn_gate)
     up_rows = half_dot(hidden_two, ffn_up)
     inner_rows = (jax.nn.silu(gate_rows) * up_rows).astype(jnp.bfloat16)
-    ffn_out = lax.psum(half_dot(inner_rows, ffn_down), "head")
-    block_output = (middle + ffn_out).reshape(seq_count, tok_rows, model_width)
+    ffn_part = half_dot(inner_rows, ffn_down)
     grad_rows = out_grad.reshape(row_count, model_width)
     grad_ffn = grad_rows.astype(jnp.bfloat16)
     ffn_down_grad = half_outer(inner_rows, grad_ffn)
@@ -396,7 +524,12 @@
     grad_gate = (grad_inner * up_rows * silu_slope(gate_rows)).astype(jnp.bfloat16)
     ffn_gate_grad = half_outer(hidden_two, grad_gate)
     ffn_up_grad = half_outer(hidden_two, grad_up)
-    grad_hidden_two = lax.psum(half_back(grad_gate, ffn_gate) + half_back(grad_up, ffn_up), "head")
+    hidden_two_part = half_back(grad_gate, ffn_gate) + half_back(grad_up, ffn_up)
+    hidden_two_part, ffn_gate_grad, ffn_up_grad, ffn_down_grad = lax.optimization_barrier(
+        (hidden_two_part, ffn_gate_grad, ffn_up_grad, ffn_down_grad)
+    )
+    ffn_grads = lax.psum((ffn_gate_grad, ffn_up_grad, ffn_down_grad), "seq")
+    grad_hidden_two = head_sum(hidden_two_part, "head", 3)
     ffn_gain_grad = jnp.sum(grad_hidden_two * normed_two, axis=0)
     grad_middle = grad_rows + rms_back(grad_hidden_two * ffn_gain, normed_two, scale_two)
     grad_mixer = grad_middle.astype(jnp.bfloat16)
@@ -409,7 +542,7 @@
         seq_count, tok_rows, value_size
     )
     state_pull = jnp.einsum("btk,btv->bvk", query_decayed, grad_mixed, precision=HIGH)
-    grad_state_out = carried_in(block_decay, state_pull, "seq", True)
+    grad_state_out = carried_in(block_decay, state_pull, "seq", True, 1)
     grad_queries, grad_keys, grad_values, grad_decay = gla_backward(
         queries, key_rows, value_rows, grad_mixed, scores, factors, states, prefix, state_in, grad_state_out
     )
@@ -449,44 +582,34 @@
         + half_back(grad_gate_raw, gate_weight)
     )
     hidden_part = hidden_part + exact_back(grad_rank, down_wide)
-    grad_hidden_one = lax.psum(hidden_part, "head")
+    down_rows = decay_down_part.size // model_width
+    tail_rows = -(-(down_rows + 1) // 32) * 32
+    tail = jnp.concatenate([decay_down_part.reshape(-1), head_gain_part])
+    tail = jnp.pad(tail, (0, tail_rows * model_width - tail.size)).reshape(tail_rows, model_width)
+    summed = head_sum(jnp.concatenate([hidden_part, ffn_part, tail], axis=0), "head", 4)
+    grad_hidden_one = summed[:row_count]
+    block_output = (middle + summed[row_count : 2 * row_count]).reshape(seq_count, tok_rows, model_width)
+    tail = summed[2 * row_count :].reshape(-1)[: decay_down_part.size + head_gain_part.size]
     attn_gain_grad = jnp.sum(grad_hidden_one * normed_one, axis=0)
     input_grad = (
         grad_middle + rms_back(grad_hidden_one * attn_gain, normed_one, scale_one)
     ).reshape(seq_count, tok_rows, model_width)
-    decay_down_grad, head_gain_grad = lax.psum((decay_down_part, head_gain_part), ("seq", "head"))
-    (
-        attn_gain_grad,
-        query_weight_grad,
-        key_weight_grad,
-        value_weight_grad,
-        gate_weight_grad,
-        decay_up_grad,
-        decay_bias_grad,
-        conv_grad,
-        out_weight_grad,
-        ffn_gain_grad,
-        ffn_gate_grad,
-        ffn_up_grad,
-        ffn_down_grad,
-    ) = lax.psum(
-        (
-            attn_gain_grad,
-            query_weight_grad,
-            key_weight_grad,
-            value_weight_grad,
-            gate_weight_grad,
-            decay_up_grad,
-            decay_bias_grad,
-            conv_grad,
-            out_weight_grad,
-            ffn_gain_grad,
-            ffn_gate_grad,
-            ffn_up_grad,
-            ffn_down_grad,
-        ),
-        "seq",
-    )
+    small = [tail, attn_gain_grad, ffn_gain_grad, decay_up_grad, decay_bias_grad, conv_grad]
+    small_row = jnp.concatenate([item.reshape(-1) for item in small])
+    small_rows = -(-small_row.size // (8 * key_size)) * 8
+    small_row = jnp.pad(small_row, (0, small_rows * key_size - small_row.size))
+    joined = jnp.concatenate([query_weight_grad, small_row.reshape(small_rows, key_size)], axis=0)
+    rest = (joined, key_weight_grad, value_weight_grad, gate_weight_grad, out_weight_grad)
+    ffn_grads, rest = lax.optimization_barrier((ffn_grads, rest))
+    joined, key_weight_grad, value_weight_grad, gate_weight_grad, out_weight_grad = lax.psum(rest, "seq")
+    ffn_gate_grad, ffn_up_grad, ffn_down_grad = ffn_grads
+    query_weight_grad = joined[:model_width]
+    small_row = joined[model_width:].reshape(-1)
+    parts, start = [], 0
+    for item in [decay_down_part, head_gain_part] + small[1:]:
+        parts.append(small_row[start : start + item.size].reshape(item.shape))
+        start += item.size
+    decay_down_grad, head_gain_grad, attn_gain_grad, ffn_gain_grad, decay_up_grad, decay_bias_grad, conv_grad = parts
     query_conv_grad = conv_grad[:, :key_size]
     key_conv_grad = conv_grad[:, key_size : 2 * key_size]
     value_conv_grad = conv_grad[:, 2 * key_size :]

time: 1120 us -> 769 us (0.69)
  waiting for transfers between devices: 837 us -> 279 us
  Pallas kernels: 23.4 us -> 294 us
  blocking collectives: 79.3 us -> 0 us
    psum x5 -> x2, waiting for transfers between devices: 742 us -> 279 us  [the longest x1 154 us: shards(): lax.psum(rest, 'seq')]
    pallas_call x0 -> x5, Pallas kernels: none -> 270 us  [the longest x3 213 us: head_sum(): pl.pallas_call(functools.partial(sum_kernel, axis), out_shape=jax.ShapeDt...]
    all_gather x2 -> x0, waiting for transfers between devices: 92.4 us -> none  [carried_in(): gathered = lax.all_gather(jnp.concatenate([state, decay], axis=1), axis)]
    psum x2 -> x0, blocking collectives: 79.3 us -> none  [the longest x1 41.6 us: shards(): lax.psum((decay_down_part, head_gain_part), ('seq', 'head'))]
    unnamed x175 -> x197, local copies, waits for them, and re-layouts: 32.1 us -> 29.4 us
  transfers between devices with their start and end apart: 9 -> 4, of which waited for: 8 -> 2; matrix products, arithmetic and copies ran while one was open for 5% -> 9% of each run, Pallas kernels for 0% -> 14%
where the time goes in v2:
time: 769 us; the launch traced here: 763 us
  Pallas kernels  294 us (38%)
  waiting for transfers between devices  279 us (36%)
  other arithmetic  61.1 us (8%)
  matrix products  61 us (8%)
  local copies, waits for them, and re-layouts  46.3 us (6%)
  between operations  15.3 us (2%)
    pallas_call x3, Pallas kernels, head_sum(): pl.pallas_call(functools.partial(sum_kernel, axis), out_shape=jax.ShapeDt...  213 us
    psum x1, waiting for transfers between devices, shards(): lax.psum(rest, 'seq')  154 us
    psum x1, waiting for transfers between devices, shards(): ffn_grads = lax.psum((ffn_gate_grad, ffn_up_grad, ffn_down_grad), 'seq')  126 us
    pallas_call x2, Pallas kernels, carried_in(): pl.pallas_call(functools.partial(prefix_kernel, axis, reverse), out_shape...  57.5 us
    unnamed x197, local copies, waits for them, and re-layouts  29.4 us
    dot_general x8, matrix products, half_outer(): lax.dot_general(left, right, (((0,), (0,)), ((), ())), preferred_element_...  17.2 us
    dot_general x8, matrix products, half_back(): lax.dot_general(left, right, (((1,), (1,)), ((), ())), preferred_element_...  16 us
    dot_general x8, matrix products, half_dot(): return jnp.dot(left, right, preferred_element_type=jnp.float32)  15.8 us
  transfers between devices with their start and end apart: 4, of which 2 were waited for; matrix products, arithmetic and copies ran while one was open for 9% of the time, Pallas kernels for 14%

profile of v2, /device:TPU:0, one launch (start us, length us, event | category | flops | bytes accessed | tf_op | source)
XLA Modules:
  0.0 763.0 jit_solution(2638842965562626218)
XLA Ops:
  7.3 2.7 multiply_reduce_fusion.5
  16.2 2.9 copy.45
  20.4 4.9 collective-permute-start
  27.4 2.6 bitcast_convert_fusion
  30.2 3.3 fusion.40
  33.4 1.7 fusion.14
  35.8 3.4 fusion.7
  40.8 13.5 %gla_local.1 = (f32[2,512,256]{2,1,0:T(8,128)S(1)}, f32[2,512,128]{2,1,0:T(8,128)S(1)}, f32[2,4,128,128]{3,2,1,0:T(8,128)S(1)}, f32[2,4,1152,128]{3,2,1,0:T(8,12...) custom-call(f32[2,512,128]{2,1,0:T(8,128)S(1)} %get-tuple-element.14, ...), custom_call_target="tpu_custom_call" | custom-call | tf_op jit(solution)/shard_map/gla_local/pallas_call | solution.py:233
  54.3 28.1 %state_prefix.2.state_in = f32[2,256,128]{2,1,0:T(8,128)S(1)} custom-call(f32[2,264,128]{2,1,0:T(8,128)S(1)} %pad_maximum_fusion.5.block), custom_call_target="tpu_custom_call" | custom-call | tf_op jit(solution)/shard_map/state_prefix/pallas_call | solution.py:349
  84.1 1.7 multiply_convert_fusion.6
  85.8 2.7 fusion.39
  88.6 53.6 %head_sum.3 = f32[4,4,64,1024]{3,2,1,0:T(8,128)S(1)} custom-call(f32[4,4,64,1024]{3,2,1,0:T(8,128)} %bitcast.165), custom_call_target="tpu_custom_call" | custom-call | tf_op jit(solution)/shard_map/head_sum/pallas_call | solution.py:425
  145.6 1.7 fusion.41
  147.4 3.4 multiply_convert_fusion.2
  150.8 3.2 fusion.50
  154.1 1.8 fusion.42
  155.9 3.2 fusion.51
  159.2 3.9 convolution_add_fusion
  163.1 3.3 fusion.43
  166.3 53.5 %head_sum.4 = f32[4,4,64,1024]{3,2,1,0:T(8,128)S(1)} custom-call(f32[4,4,64,1024]{3,2,1,0:T(8,128)} %bitcast.174), custom_call_target="tpu_custom_call" | custom-call | tf_op jit(solution)/shard_map/head_sum/pallas_call | solution.py:425
  219.9 2.0 copy-done.3
  222.0 6.9 multiply_reduce_fusion
  228.9 6.8 fusion.2
  235.8 1.9 multiply_reduce_fusion.11
  239.3 1.9 fusion.44
  241.1 29.4 %state_prefix.3.grad_last = f32[2,256,128]{2,1,0:T(8,128)S(1)} custom-call(f32[2,264,128]{2,1,0:T(8,128)S(1)} %pad_maximum_fusion.4.block), custom_call_target="tpu_custom_call" | custom-call | tf_op jit(solution)/shard_map/state_prefix/pallas_call | solution.py:349
  270.7 9.9 %gla_back.1 = (f32[2,512,128]{2,1,0:T(8,128)S(1)}, f32[2,512,128]{2,1,0:T(8,128)S(1)}, f32[2,512,256]{2,1,0:T(8,128)S(1)}, f32[2,512,128]{2,1,0:T(8,128)S(1)}) custom-call(f32[2,512,128]{2,1,0:T(8,128)S(1)} %get-tuple-element.142.query, f32[2,512,128]{2,1,0:T(8,128)S(1)} %get-tuple-element.141.key, f32[2,512,256]{2,1,0:T(8,128)} %slice.169.value, ...), custom_call_target="tpu_custom_call" | custom-call | tf_op jit(solution)/shard_map/gla_back/pallas_call | solution.py:276
  282.2 2.3 multiply_reduce_fusion.9
  292.3 2.3 fusion.48
  295.8 6.3 pad_add_fusion
  302.2 1.7 fusion.49
  303.9 2.9 fusion.45
  307.7 1.7 fusion.8
  310.0 3.9 fusion.47
  314.6 1.9 fusion.6
  320.8 3.0 add_add_fusion
  323.9 3.9 pad_maximum_fusion
  327.8 105.4 %head_sum.5 = f32[5,4,104,1024]{3,2,1,0:T(8,128)} custom-call(f32[5,4,104,1024]{3,2,1,0:T(8,128)} %bitcast.161), custom_call_target="tpu_custom_call" | custom-call | tf_op jit(solution)/shard_map/head_sum/pallas_call | solution.py:425
  434.3 3.7 multiply_reduce_fusion.1
  439.7 1.6 fusion.19
  441.3 1.7 fusion.15
  443.0 125.7 %all-reduce.14.cloned.1.call-done = (f32[1024,704]{0,1:T(8,128)}, f32[1024,704]{0,1:T(8,128)}, f32[704,1024]{1,0:T(8,128)}) async-done(((f32[1024,704]{0,1:T(8,128)}, f32[1024,704]{0,1:T(8,128)}, f32[704,1024]{1,0:T(8,128)}), (f32[1024,704]{0,1:T(8,128)}, f32[1024,704]{0,1:T(8,128)}, f32[704,1024]{1,0:T(8,128)})) %all-reduce.14.cloned.1.call-update) | async-done | bytes 8650768 | tf_op jit(solution)/shard_map/psum | solution.py:531
  568.8 11.7 %multiply_add_fusion = (f32[1024,1024]{1,0:T(8,128)}, f32[1024,1024]{1,0:T(8,128)}) fusion(f32[1024,1024]{1,0:T(8,128)} %copy-done.18, f32[2080,1024]{1,0:T(8,128)} %bitcast.160, f32[2,512,1024]{2,1,0:T(8,128)} %param.23, f32[1024]{0:T(1024)S(1)} %broadcast_multiply_fusion.7, f32[1024]{0:T(1024)S(1)} %copy-done.64, f32[1024]{0:T(1024)S(1)} %bitcast.180, ...), kind=kLoop, calls=%fused_computation.11 | loop fusion | flops 8388608 | bytes 29372416 | tf_op jit(solution)/shard_map/add | solution.py:595
  580.5 153.5 %all-reduce.12.cloned.1.call-done = (f32[1208,128]{1,0:T(8,128)}, f32[1024,128]{1,0:T(8,128)}, f32[1024,256]{1,0:T(8,128)}, f32[1024,256]{1,0:T(8,128)}, f32[256,1024]{1,0:T(8,128)}) async-done(((f32[1208,128]{1,0:T(8,128)}, f32[1024,128]{1,0:T(8,128)}, f32[1024,256]{1,0:T(8,128)}, f32[1024,256]{1,0:T(8,128)}, f32[256,1024]{1,0:T(8,128)}), (f32[1208,128]{1,0:T(8,128)}, f32[1024,128]{1,0:T(8,128)}, ...) | async-done | bytes 4288528 | tf_op jit(solution)/shard_map/psum | solution.py:604
  734.9 1.9 slice.179
  748.6 1.6 copy.76
  751.5 1.6 copy.77
  754.3 1.6 copy.78
  (253 shorter events, 53.8 us)
Async XLA Ops:
  7.2 140.1 %copy-start = (bf16[1024,704]{0,1:T(8,128)(2,1)S(1)}, bf16[1024,704]{0,1:T(8,128)(2,1)}, u32[]{:S(2)}) copy-start(bf16[1024,704]{0,1:T(8,128)(2,1)} %param.39) | copy-start | bytes 4325380
  7.2 561.5 %all-reduce.14.cloned.1.call-start = ((), (), s32[]{:S(2)}) async-start(), calls=%async_computation.1 | async-start | bytes 17301504 | tf_op jit(solution)/shard_map/psum | solution.py:531
  7.3 3.5 copy-start.12
  11.8 14.2 %copy-start.15 = (bf16[1024,1024]{1,0:T(8,128)(2,1)}, bf16[1024,1024]{1,0:T(8,128)(2,1)S(1)}, u32[]{:S(2)}) copy-start(bf16[1024,1024]{1,0:T(8,128)(2,1)S(1)} %multiply_convert_fusion.1) | copy-start | bytes 6291460
  20.4 15.3 %collective-permute-start = (f32[2,3,512]{2,1,0:T(4,128)}, f32[2,3,512]{2,1,0:T(4,128)S(1)}, u32[]{:S(2)}, u32[]{:S(2)}) collective-permute-start(f32[2,3,512]{2,1,0:T(4,128)} %slice.159), channel_id=1, source_target_pairs={{0,4},{4,8},{8,12},{12,16},{16,20},{20,24},{24,28},{1,5},{5,9},{9,... | collective-permute-start | bytes 36872 | tf_op jit(solution)/shard_map/ppermute | solution.py:18
  27.4 6.0 copy-start.56
  30.1 3.4 copy-start.37
  30.1 3.3 copy-start.75
  30.1 3.3 copy-start.84
  30.2 5.6 copy-start.20
  54.3 29.4 %copy-start.6 = (f32[2,4,256,128]{3,2,1,0:T(8,128)}, f32[2,4,256,128]{3,2,1,0:T(8,128)S(1)}, u32[]{:S(2)}) copy-start(f32[2,4,256,128]{3,2,1,0:T(8,128)S(1)} %get-tuple-element.50.states) | copy-start | bytes 3145732
  54.3 29.4 %copy-start.7 = (f32[2,4,128,128]{3,2,1,0:T(8,128)}, f32[2,4,128,128]{3,2,1,0:T(8,128)S(1)}, u32[]{:S(2)}) copy-start(f32[2,4,128,128]{3,2,1,0:T(8,128)S(1)} %get-tuple-element.48.scores_in) | copy-start | bytes 1572868
  88.6 53.7 %copy-start.13 = (f32[2,512,1024]{2,1,0:T(8,128)S(1)}, f32[2,512,1024]{2,1,0:T(8,128)}, u32[]{:S(2)}) copy-start(f32[2,512,1024]{2,1,0:T(8,128)} %param.23) | copy-start | bytes 12582916
  150.8 12.3 %copy-start.86 = (bf16[1024,704]{0,1:T(8,128)(2,1)}, bf16[1024,704]{0,1:T(8,128)(2,1)S(1)}, u32[]{:S(2)}) copy-start(bf16[1024,704]{0,1:T(8,128)(2,1)S(1)} %get-tuple-element.132) | copy-start | bytes 4325380
  159.2 3.9 copy-start.38
  228.9 6.9 copy-start.30
  228.9 6.9 copy-start.45
  228.9 6.9 copy-start.52
  239.2 31.4 %copy-start.27 = (f32[1024,256]{1,0:T(8,128)}, f32[1024,256]{1,0:T(8,128)S(1)}, u32[]{:S(2)}) copy-start(f32[1024,256]{1,0:T(8,128)S(1)} %get-tuple-element.136) | copy-start | bytes 3145732
  239.2 31.4 %copy-start.5 = (f32[7,128,128]{2,1,0:T(8,128)S(1)}, f32[7,128,128]{2,1,0:T(8,128)}, u32[]{:S(2)}) copy-start(f32[7,128,128]{2,1,0:T(8,128)} %constant.44.clone.masks) | copy-start | bytes 1376260
  239.2 31.4 %copy-start.8 = (f32[2,4,128,128]{3,2,1,0:T(8,128)S(1)}, f32[2,4,128,128]{3,2,1,0:T(8,128)}, u32[]{:S(2)}) copy-start(f32[2,4,128,128]{3,2,1,0:T(8,128)} %copy-done.7) | copy-start | bytes 1572868
  239.2 31.4 %copy-start.11 = (bf16[128,128]{1,0:T(8,128)(2,1)S(1)}, bf16[128,128]{1,0:T(8,128)(2,1)}, u32[]{:S(2)}) copy-start(bf16[128,128]{1,0:T(8,128)(2,1)} %constant.45.clone.suffix) | copy-start | bytes 98308
  270.6 10.0 %copy-start.28 = (f32[2,512,512]{2,1,0:T(8,128)S(1)}, f32[2,512,512]{2,1,0:T(8,128)}, u32[]{:S(2)}) copy-start(f32[2,512,512]{2,1,0:T(8,128)} %get-tuple-element.129) | copy-start | bytes 6291460
  285.6 3.3 copy-start.25
  288.9 3.1 copy-start.76
  288.9 25.7 %collective-permute-start.1 = (f32[2,3,512]{2,1,0:T(4,128)}, f32[2,3,512]{2,1,0:T(4,128)}, u32[]{:S(2)}, u32[]{:S(2)}) collective-permute-start(f32[2,3,512]{2,1,0:T(4,128)} %pad_add_fusion.1), channel_id=1, source_target_pairs={{4,0},{8,4},{12,8},{16,12},{20,16},{24,20},{28,24},{5,1},{9,5},{13... | collective-permute-start | bytes 36872 | tf_op jit(solution)/shard_map/ppermute | solution.py:18
  290.4 443.6 %all-reduce.12.cloned.1.call-start = ((), (), s32[]{:S(2)}) async-start(), calls=%async_computation | async-start | bytes 8577024 | tf_op jit(solution)/shard_map/psum | solution.py:604
  292.0 3.5 copy-start.57
  295.8 6.3 copy-start.41
  303.9 3.6 copy-start.19
  303.9 3.9 copy-start.33
  310.0 3.9 copy-start.58
  310.0 3.9 copy-start.79
  310.0 3.9 copy-start.71
  310.0 3.9 copy-start.72
  310.0 3.9 copy-start.73
  310.0 3.9 copy-start.74
  320.8 3.0 copy-start.31
  320.8 3.0 copy-start.50
  327.8 106.4 %copy-start.60 = (f32[22912]{0:T(1024)S(1)}, f32[22912]{0:T(1024)}, u32[]{:S(2)}) copy-start(f32[22912]{0:T(1024)} %custom-call) | copy-start | bytes 274948
  327.8 106.4 %copy-start.14 = (f32[2,512,1024]{2,1,0:T(8,128)S(1)}, f32[2,512,1024]{2,1,0:T(8,128)}, u32[]{:S(2)}) copy-start(f32[2,512,1024]{2,1,0:T(8,128)} %param.23) | copy-start | bytes 12582916
  327.8 106.5 %copy-start.62 = (f32[1,4,2,128]{3,1,2,0:T(4,128)S(1)}, f32[1,4,2,128]{3,1,2,0:T(4,128)}, u32[]{:S(2)}) copy-start(f32[1,4,2,128]{3,1,2,0:T(4,128)} %copy-done.61) | copy-start | bytes 12292
  327.8 106.5 %copy-start.64 = (f32[1024]{0:T(1024)S(1)}, f32[1024]{0:T(1024)}, u32[]{:S(2)}) copy-start(f32[1024]{0:T(1024)} %param.24) | copy-start | bytes 12292
  434.3 3.8 copy-start.70
  734.0 10.2 %copy-start.55 = (f32[1024,128]{1,0:T(8,128)S(1)}, f32[1024,128]{1,0:T(8,128)}, u32[]{:S(2)}) copy-start(f32[1024,128]{1,0:T(8,128)} %get-tuple-element.166) | copy-start | bytes 1572868
  734.0 11.0 %copy-start.44 = (f32[1024,256]{1,0:T(8,128)S(1)}, f32[1024,256]{1,0:T(8,128)}, u32[]{:S(2)}) copy-start(f32[1024,256]{1,0:T(8,128)} %get-tuple-element.167) | copy-start | bytes 3145732
  748.6 2.9 copy-start.35
  751.5 4.4 copy-start.1
  (44 other events, 86.1 us)
Sparse Core Ops, SparseCore 0:
  290.5 278.2 all-reduce.13
  574.7 159.1 all-reduce.11

commit v3 on v2

--- a/solution.py
+++ b/solution.py
@@ -10,6 +10,8 @@
 
 EPS = 1e-06
 HIGH = lax.Precision.HIGHEST
+MESH = pl.DeviceIdType.MESH
+QUICK = pl.CostEstimate(flops=1, bytes_accessed=1, transcendentals=0)
 
 
 def shifted(value, axis, steps):
@@ -249,6 +251,7 @@
             jax.ShapeDtypeStruct((seqs, 8, width), f32),
         ],
         scratch_shapes=[pltpu.VMEM((seqs, values, width), f32), pltpu.VMEM((seqs, 8, width), f32)],
+        cost_estimate=QUICK,
         compiler_params=pltpu.CompilerParams(vmem_limit_bytes=48 * 1024 * 1024),
         name="gla_local",
     )(query, key, value, decay, jnp.asarray(spans, jnp.bfloat16), jnp.asarray(masks))
@@ -289,13 +292,11 @@
             jax.ShapeDtypeStruct((seqs, count, width), f32),
         ],
         scratch_shapes=[pltpu.VMEM((seqs, values, width), f32)],
+        cost_estimate=QUICK,
         compiler_params=pltpu.CompilerParams(vmem_limit_bytes=48 * 1024 * 1024),
         name="gla_back",
     )(query, key, value, grad, scores, factors, states, prefix, state_in, grad_last,
       jnp.asarray(masks), jnp.asarray(suffix, jnp.bfloat16))
-
-
-MESH = pl.DeviceIdType.MESH
 
 
 def greet(axis, partners):
@@ -352,6 +353,7 @@
         in_specs=[pl.BlockSpec(memory_space=pltpu.VMEM)],
         out_specs=pl.BlockSpec(memory_space=pltpu.VMEM),
         scratch_shapes=[slots, slots, pltpu.SemaphoreType.DMA((steps,)), pltpu.SemaphoreType.DMA((steps,))],
+        cost_estimate=QUICK,
         compiler_params=pltpu.CompilerParams(
             collective_id=call_id, has_side_effects=True, vmem_limit_bytes=32 * 1024 * 1024
         ),
@@ -434,12 +436,100 @@
             pltpu.SemaphoreType.DMA((5, pieces)),
             pltpu.SemaphoreType.DMA((5, pieces)),
         ],
+        cost_estimate=QUICK,
         compiler_params=pltpu.CompilerParams(
             collective_id=call_id, has_side_effects=True, vmem_limit_bytes=48 * 1024 * 1024
         ),
         name="head_sum",
     )(terms.reshape(pieces, 4, deep, columns))
     return out.reshape(rows, columns)
+
+
+def seq_sum_kernel(axis, terms, out, *scratch):
+    pieces, count = terms.shape[:2]
+    steps = count.bit_length() - 1
+    received, partial = scratch[:steps], scratch[steps : 2 * steps - 1]
+    send_sem, recv_sem = scratch[2 * steps - 1 :]
+    me = lax.axis_index(axis)
+    bits = [(me // (1 << step)) % 2 for step in range(steps)]
+    partners = [me + (1 << step) * (1 - 2 * bit) for step, bit in enumerate(bits)]
+    starts = [0]
+    for step, bit in enumerate(bits):
+        starts.append(starts[-1] + bit * (count >> (step + 1)))
+    greet(axis, partners)
+
+    def copy(slot, step, piece, source, target):
+        return pltpu.make_async_remote_copy(
+            src_ref=source,
+            dst_ref=target,
+            send_sem=send_sem.at[slot, piece],
+            recv_sem=recv_sem.at[slot, piece],
+            device_id={axis: partners[step]},
+            device_id_type=MESH,
+        )
+
+    def down(step, piece):
+        half = count >> (step + 1)
+        held = terms if step == 0 else partial[step - 1]
+        return copy(
+            step, step, piece, held.at[piece, pl.ds((1 - bits[step]) * half, half)], received[step].at[piece]
+        )
+
+    def up(step, piece):
+        half = count >> (step + 1)
+        place = out.at[piece, pl.ds(starts[step + 1], half)]
+        return copy(steps + step, step, piece, place, place)
+
+    for piece in range(pieces):
+        down(0, piece).start()
+    for step in range(steps):
+        half = count >> (step + 1)
+        held = terms if step == 0 else partial[step - 1]
+        for piece in range(pieces):
+            down(step, piece).wait_recv()
+            kept = held[piece, pl.ds(bits[step] * half, half)] + received[step][piece]
+            if step + 1 < steps:
+                partial[step][piece] = kept
+                down(step + 1, piece).start()
+            else:
+                out[piece, pl.ds(starts[steps], 1)] = kept
+                up(step, piece).start()
+    for step in range(steps - 1, -1, -1):
+        for piece in range(pieces):
+            up(step, piece).wait_recv()
+            if step:
+                up(step - 1, piece).start()
+    for step in range(steps):
+        for piece in range(pieces):
+            down(step, piece).wait_send()
+            up(step, piece).wait_send()
+
+
+def seq_sum(terms, axis, call_id, pieces=3):
+    rows, columns = terms.shape
+    count = lax.axis_size(axis)
+    steps = count.bit_length() - 1
+    assert count == 1 << steps
+    deep = -(-rows // (8 * pieces * count)) * 8
+    shape = (pieces, count, deep, columns)
+    padded = jnp.pad(terms, ((0, pieces * count * deep - rows), (0, 0)))
+    f32 = jnp.float32
+    slots = [pltpu.VMEM((pieces, count >> (step + 1), deep, columns), f32) for step in range(steps)]
+    out = pl.pallas_call(
+        functools.partial(seq_sum_kernel, axis),
+        out_shape=jax.ShapeDtypeStruct(shape, f32),
+        in_specs=[pl.BlockSpec(memory_space=pltpu.VMEM)],
+        out_specs=pl.BlockSpec(memory_space=pltpu.VMEM),
+        scratch_shapes=slots
+        + slots[: steps - 1]
+        + [pltpu.SemaphoreType.DMA((2 * steps, pieces)), pltpu.SemaphoreType.DMA((2 * steps, pieces))],
+        cost_estimate=QUICK,
+        compiler_params=pltpu.CompilerParams(
+            collective_id=call_id, has_side_effects=True, vmem_limit_bytes=48 * 1024 * 1024
+        ),
+        name="seq_sum",
+    )(padded.reshape(shape))
+    return out.reshape(pieces * count * deep, columns)[:rows]
 
 
 def shards(
@@ -596,14 +686,21 @@
     ).reshape(seq_count, tok_rows, model_width)
     small = [tail, attn_gain_grad, ffn_gain_grad, decay_up_grad, decay_bias_grad, conv_grad]
     small_row = jnp.concatenate([item.reshape(-1) for item in small])
-    small_rows = -(-small_row.size // (8 * key_size)) * 8
-    small_row = jnp.pad(small_row, (0, small_rows * key_size - small_row.size))
-    joined = jnp.concatenate([query_weight_grad, small_row.reshape(small_rows, key_size)], axis=0)
-    rest = (joined, key_weight_grad, value_weight_grad, gate_weight_grad, out_weight_grad)
-    ffn_grads, rest = lax.optimization_barrier((ffn_grads, rest))
-    joined, key_weight_grad, value_weight_grad, gate_weight_grad, out_weight_grad = lax.psum(rest, "seq")
+    out_side = out_weight_grad.reshape(model_width, -1)
+    joined = jnp.concatenate(
+        [query_weight_grad, key_weight_grad, value_weight_grad, gate_weight_grad, out_side], axis=1
+    )
+    wide = joined.shape[1]
+    small_rows = -(-small_row.size // wide)
+    small_row = jnp.pad(small_row, (0, small_rows * wide - small_row.size))
+    joined = jnp.concatenate([joined, small_row.reshape(small_rows, wide)], axis=0)
+    joined = seq_sum(joined, "seq", 5)
     ffn_gate_grad, ffn_up_grad, ffn_down_grad = ffn_grads
-    query_weight_grad = joined[:model_width]
+    query_weight_grad = joined[:model_width, :key_size]
+    key_weight_grad = joined[:model_width, key_size : 2 * key_size]
+    value_weight_grad = joined[:model_width, 2 * key_size : 2 * key_size + value_size]
+    gate_weight_grad = joined[:model_width, 2 * key_size + value_size : 2 * (key_size + value_size)]
+    out_weight_grad = joined[:model_width, 2 * (key_size + value_size) :].reshape(out_weight.shape)
     small_row = joined[model_width:].reshape(-1)
     parts, start = [], 0
     for item in [decay_down_part, head_gain_part] + small[1:]:

time: 769 us -> 736 us (0.957)
  waiting for transfers between devices: 279 us -> 0.02 us
  Pallas kernels: 294 us -> 535 us
  local copies, waits for them, and re-layouts: 46.3 us -> 61.7 us
    pallas_call x0 -> x1, Pallas kernels: none -> 242 us  [seq_sum(): pl.pallas_call(functools.partial(seq_sum_kernel, axis), out_shape=jax.Sha...]
    psum x1 -> x0, waiting for transfers between devices: 154 us -> none  [shards(): lax.psum(rest, 'seq')]
    psum x1, waiting for transfers between devices: 126 us -> 0.01 us  [shards(): ffn_grads = lax.psum((ffn_gate_grad, ffn_up_grad, ffn_down_grad), 'seq')]
    unnamed x197 -> x192, local copies, waits for them, and re-layouts: 29.4 us -> 35.4 us
  transfers between devices with their start and end apart: 4 -> 3, of which waited for: 2 -> 0; matrix products, arithmetic and copies ran while one was open for 9% -> 10% of each run, Pallas kernels for 14% -> 47%
where the time goes in v3:
time: 736 us; the launch traced here: 730 us
  Pallas kernels  535 us (73%)
  local copies, waits for them, and re-layouts  61.7 us (8%)
  other arithmetic  56.3 us (8%)
  matrix products  55.9 us (8%)
  between operations  15.5 us (2%)
    pallas_call x1, Pallas kernels, seq_sum(): pl.pallas_call(functools.partial(seq_sum_kernel, axis), out_shape=jax.Sha...  242 us
    pallas_call x3, Pallas kernels, head_sum(): pl.pallas_call(functools.partial(sum_kernel, axis), out_shape=jax.ShapeDt...  212 us
    pallas_call x2, Pallas kernels, carried_in(): pl.pallas_call(functools.partial(prefix_kernel, axis, reverse), out_shape...  57.5 us
    unnamed x192, local copies, waits for them, and re-layouts  35.4 us
    dot_general x8, matrix products, half_dot(): return jnp.dot(left, right, preferred_element_type=jnp.float32)  15.5 us
    dot_general x8, matrix products, half_back(): lax.dot_general(left, right, (((1,), (1,)), ((), ())), preferred_element_...  14.9 us
  transfers between devices with their start and end apart: 3, of which 0 were waited for; matrix products, arithmetic and copies ran while one was open for 10% of the time, Pallas kernels for 47%

profile of v3, /device:TPU:0, one launch (start us, length us, event | category | flops | bytes accessed | tf_op | source)
XLA Modules:
  0.0 730.5 jit_solution(708378627699669649)
XLA Ops:
  7.3 2.7 multiply_reduce_fusion.5
  16.2 2.9 copy.45
  19.9 4.9 collective-permute-start
  26.2 2.6 bitcast_convert_fusion
  28.9 3.3 fusion.39
  33.8 2.5 fusion.7
  37.6 13.5 %gla_local.1 = (f32[2,512,256]{2,1,0:T(8,128)S(1)}, f32[2,512,128]{2,1,0:T(8,128)S(1)}, f32[2,4,128,128]{3,2,1,0:T(8,128)S(1)}, f32[2,4,1152,128]{3,2,1,0:T(8,12...) custom-call(f32[2,512,128]{2,1,0:T(8,128)S(1)} %get-tuple-element.10, ...), custom_call_target="tpu_custom_call" | custom-call | flops 1 | bytes 1 | tf_op jit(solution)/shard_map/gla_local/pallas_call | solution.py:235
  54.5 28.1 %state_prefix.2.state_in = f32[2,256,128]{2,1,0:T(8,128)S(1)} custom-call(f32[2,264,128]{2,1,0:T(8,128)S(1)} %pad_maximum_fusion.5.block), custom_call_target="tpu_custom_call" | custom-call | flops 1 | bytes 1 | tf_op jit(solution)/shard_map/state_prefix/pallas_call | solution.py:350
  84.3 1.8 multiply_convert_fusion.6
  86.0 2.7 fusion.38
  88.8 53.6 %head_sum.3 = f32[4,4,64,1024]{3,2,1,0:T(8,128)S(1)} custom-call(f32[4,4,64,1024]{3,2,1,0:T(8,128)} %bitcast.161), custom_call_target="tpu_custom_call" | custom-call | flops 1 | bytes 1 | tf_op jit(solution)/shard_map/head_sum/pallas_call | solution.py:427
  145.8 1.7 fusion.40
  147.6 3.1 multiply_convert_fusion.2
  150.7 1.8 fusion.41
  152.6 3.2 fusion.48
  155.8 3.2 fusion.49
  159.1 3.9 convolution_add_fusion
  163.0 3.3 fusion.42
  166.2 53.5 %head_sum.4 = f32[4,4,64,1024]{3,2,1,0:T(8,128)S(1)} custom-call(f32[4,4,64,1024]{3,2,1,0:T(8,128)} %bitcast.171), custom_call_target="tpu_custom_call" | custom-call | flops 1 | bytes 1 | tf_op jit(solution)/shard_map/head_sum/pallas_call | solution.py:427
  219.8 2.0 copy-done.3
  221.9 6.3 multiply_reduce_fusion
  228.2 7.1 fusion.2
  237.8 1.9 fusion.43
  239.8 3.9 fusion.46
  243.7 29.4 %state_prefix.3.grad_last = f32[2,256,128]{2,1,0:T(8,128)S(1)} custom-call(f32[2,264,128]{2,1,0:T(8,128)S(1)} %pad_maximum_fusion.4.block), custom_call_target="tpu_custom_call" | custom-call | flops 1 | bytes 1 | tf_op jit(solution)/shard_map/state_prefix/pallas_call | solution.py:350
  273.1 9.9 %gla_back.1 = (f32[2,512,128]{2,1,0:T(8,128)S(1)}, f32[2,512,128]{2,1,0:T(8,128)S(1)}, f32[2,512,256]{2,1,0:T(8,128)S(1)}, f32[2,512,128]{2,1,0:T(8,128)S(1)}) custom-call(f32[2,512,128]{2,1,0:T(8,128)S(1)} %get-tuple-element.107.query, f32[2,512,128]{2,1,0:T(8,128)S(1)} %get-tuple-element.106.key, f32[2,512,256]{2,1,0:T(8,128)} %slice.175.value, ...), custom_call_target="tpu_custom_call" | custom-call | flops 1 | bytes 1 | tf_op jit(solution)/shard_map/gla_back/pallas_call | solution.py:279
  284.7 1.8 multiply_reduce_fusion.9
  287.6 2.4 pad_add_fusion
  292.6 1.7 fusion.8
  294.3 2.3 fusion.47
  299.3 2.7 fusion.44
  302.7 1.8 reshape.251
  305.8 1.9 fusion.6
  311.9 2.8 add_add_fusion
  314.7 4.2 pad_maximum_fusion
  318.9 105.1 %head_sum.5 = f32[5,4,104,1024]{3,2,1,0:T(8,128)} custom-call(f32[5,4,104,1024]{3,2,1,0:T(8,128)} %bitcast.157), custom_call_target="tpu_custom_call" | custom-call | flops 1 | bytes 1 | tf_op jit(solution)/shard_map/head_sum/pallas_call | solution.py:427
  425.1 3.5 multiply_reduce_fusion.1
  434.1 2.6 pad_maximum_fusion.1
  436.7 5.9 copy.54
  442.7 5.7 pad.39.clone
  448.3 241.8 %seq_sum.1 = f32[3,8,48,1024]{3,2,1,0:T(8,128)S(1)} custom-call(f32[3,8,48,1024]{3,2,1,0:T(8,128)} %bitcast.162), custom_call_target="tpu_custom_call" | custom-call | flops 1 | bytes 1 | tf_op jit(solution)/shard_map/seq_sum/pallas_call | solution.py:518
  690.1 2.2 copy-done.4
  695.7 3.4 fusion.27
  701.5 2.2 fusion.28
  703.8 11.3 %multiply_add_fusion = (f32[1024,1024]{1,0:T(8,128)}, f32[1024,1024]{1,0:T(8,128)}) fusion(f32[1024,1024]{1,0:T(8,128)} %copy-done.22, f32[2080,1024]{1,0:T(8,128)} %bitcast.156, f32[2,512,1024]{2,1,0:T(8,128)} %param.23, f32[1024]{0:T(1024)S(1)} %broadcast_multiply_fusion.7, f32[1024]{0:T(1024)S(1)} %copy-done.63, f32[1024]{0:T(1024)S(1)} %bitcast.177, ...), kind=kLoop, calls=%fused_computation.12 | loop fusion | flops 8388608 | bytes 29372416 | tf_op jit(solution)/shard_map/add | solution.py:685
  715.1 3.9 copy.75
  719.0 1.6 copy.76
  721.8 1.6 copy.77
  (258 shorter events, 49.8 us)
Async XLA Ops:
  7.2 140.3 %copy-start = (bf16[1024,704]{0,1:T(8,128)(2,1)S(1)}, bf16[1024,704]{0,1:T(8,128)(2,1)}, u32[]{:S(2)}) copy-start(bf16[1024,704]{0,1:T(8,128)(2,1)} %param.39) | copy-start | bytes 4325380
  7.2 2.8 copy-start.62
  7.2 707.8 %all-reduce.11.cloned.1.call-start = ((), (), s32[]{:S(2)}) async-start(), calls=%async_computation | async-start | bytes 17301504 | tf_op jit(solution)/shard_map/psum | solution.py:621
  7.3 3.5 copy-start.16
  11.8 12.9 %copy-start.19 = (bf16[1024,1024]{1,0:T(8,128)(2,1)}, bf16[1024,1024]{1,0:T(8,128)(2,1)S(1)}, u32[]{:S(2)}) copy-start(bf16[1024,1024]{1,0:T(8,128)(2,1)S(1)} %multiply_convert_fusion.1) | copy-start | bytes 6291460
  16.2 8.5 %copy-start.76 = (f32[4,128]{1,0:T(4,128)S(1)}, f32[4,128]{1,0:T(4,128)}, u32[]{:S(2)}) copy-start(f32[4,128]{1,0:T(4,128)} %param.32) | copy-start | bytes 6148
  19.9 14.0 %collective-permute-start = (f32[2,3,512]{2,1,0:T(4,128)S(1)}, f32[2,3,512]{2,1,0:T(4,128)S(1)}, u32[]{:S(2)}, u32[]{:S(2)}) collective-permute-start(f32[2,3,512]{2,1,0:T(4,128)S(1)} %slice.165), channel_id=1, source_target_pairs={{0,4},{4,8},{8,12},{12,16},{16,20},{20,24},{24,28},{1,5},{5,9},{9,... | collective-permute-start | bytes 36872 | tf_op jit(solution)/shard_map/ppermute | solution.py:20
  26.2 6.0 copy-start.54
  26.2 2.7 copy-start.77
  26.2 2.7 copy-start.75
  26.2 2.7 copy-start.81
  28.8 3.4 copy-start.36
  28.9 3.3 copy-start.73
  28.9 3.3 copy-start.83
  28.9 4.9 copy-start.23
  33.8 2.6 copy-start.65
  33.8 2.6 copy-start.67
  33.8 2.6 copy-start.69
  33.8 2.6 copy-start.71
  33.8 2.5 copy-start.58
  54.5 29.2 %copy-start.9 = (f32[2,512,256]{2,1,0:T(8,128)S(1)}, f32[2,512,256]{2,1,0:T(8,128)}, u32[]{:S(2)}) copy-start(f32[2,512,256]{2,1,0:T(8,128)} %copy-done.8) | copy-start | bytes 3145732
  86.0 2.7 copy-start.32
  88.8 53.7 %copy-start.17 = (f32[2,512,1024]{2,1,0:T(8,128)S(1)}, f32[2,512,1024]{2,1,0:T(8,128)}, u32[]{:S(2)}) copy-start(f32[2,512,1024]{2,1,0:T(8,128)} %param.23) | copy-start | bytes 12582916
  150.7 12.3 %copy-start.85 = (bf16[1024,704]{0,1:T(8,128)(2,1)}, bf16[1024,704]{0,1:T(8,128)(2,1)S(1)}, u32[]{:S(2)}) copy-start(bf16[1024,704]{0,1:T(8,128)(2,1)S(1)} %get-tuple-element.92) | copy-start | bytes 4325380
  159.1 3.9 copy-start.37
  228.2 7.1 copy-start.30
  228.2 7.1 copy-start.43
  228.2 7.1 copy-start.50
  235.3 57.2 %copy-start.22 = (f32[1024,1024]{1,0:T(8,128)}, f32[1024,1024]{1,0:T(8,128)S(1)}, u32[]{:S(2)}) copy-start(f32[1024,1024]{1,0:T(8,128)S(1)} %fusion.2) | copy-start | bytes 12582916
  236.4 3.4 copy-start.86
  237.8 5.8 copy-start.26
  239.8 33.3 %copy-start.6 = (f32[7,128,128]{2,1,0:T(8,128)S(1)}, f32[7,128,128]{2,1,0:T(8,128)}, u32[]{:S(2)}) copy-start(f32[7,128,128]{2,1,0:T(8,128)} %constant.44.clone.masks) | copy-start | bytes 1376260
  239.8 33.3 %copy-start.11 = (f32[2,4,128,128]{3,2,1,0:T(8,128)S(1)}, f32[2,4,128,128]{3,2,1,0:T(8,128)}, u32[]{:S(2)}) copy-start(f32[2,4,128,128]{3,2,1,0:T(8,128)} %copy-done.10) | copy-start | bytes 1572868
  239.8 33.3 %copy-start.13 = (bf16[128,128]{1,0:T(8,128)(2,1)S(1)}, bf16[128,128]{1,0:T(8,128)(2,1)}, u32[]{:S(2)}) copy-start(bf16[128,128]{1,0:T(8,128)(2,1)} %constant.45.clone.suffix) | copy-start | bytes 98308
  239.8 33.3 %copy-start.15 = (f32[2,4,8,128]{3,2,1,0:T(8,128)S(1)}, f32[2,4,8,128]{3,2,1,0:T(8,128)}, u32[]{:S(2)}) copy-start(f32[2,4,8,128]{3,2,1,0:T(8,128)} %copy-done.14) | copy-start | bytes 98308
  273.1 10.1 %copy-start.27 = (f32[2,512,512]{2,1,0:T(8,128)S(1)}, f32[2,512,512]{2,1,0:T(8,128)}, u32[]{:S(2)}) copy-start(f32[2,512,512]{2,1,0:T(8,128)} %get-tuple-element.89) | copy-start | bytes 6291460
  273.1 10.1 %copy-start.59 = (f32[2,3,512]{2,1,0:T(4,128)S(1)}, f32[2,3,512]{2,1,0:T(4,128)}, u32[]{:S(2)}) copy-start(f32[2,3,512]{2,1,0:T(4,128)} %copy-done.58) | copy-start | bytes 36868
  296.7 9.0 %collective-permute-start.1 = (f32[2,3,512]{2,1,0:T(4,128)}, f32[2,3,512]{2,1,0:T(4,128)}, u32[]{:S(2)}, u32[]{:S(2)}) collective-permute-start(f32[2,3,512]{2,1,0:T(4,128)} %pad_add_fusion.1), channel_id=1, source_target_pairs={{4,0},{8,4},{12,8},{16,12},{20,16},{24,20},{28,24},{5,1},{9,5},{13... | collective-permute-start | bytes 36872 | tf_op jit(solution)/shard_map/ppermute | solution.py:20
  311.9 2.8 copy-start.31
  311.9 2.8 copy-start.48
  318.9 106.1 %copy-start.57 = (f32[22912]{0:T(1024)S(1)}, f32[22912]{0:T(1024)}, u32[]{:S(2)}) copy-start(f32[22912]{0:T(1024)} %custom-call) | copy-start | bytes 274948
  318.9 106.1 %copy-start.18 = (f32[2,512,1024]{2,1,0:T(8,128)S(1)}, f32[2,512,1024]{2,1,0:T(8,128)}, u32[]{:S(2)}) copy-start(f32[2,512,1024]{2,1,0:T(8,128)} %param.23) | copy-start | bytes 12582916
  318.9 106.1 %copy-start.61 = (f32[1,4,2,128]{3,1,2,0:T(4,128)S(1)}, f32[1,4,2,128]{3,1,2,0:T(4,128)}, u32[]{:S(2)}) copy-start(f32[1,4,2,128]{3,1,2,0:T(4,128)} %copy-done.60) | copy-start | bytes 12292
  318.9 106.1 %copy-start.63 = (f32[1024]{0:T(1024)S(1)}, f32[1024]{0:T(1024)}, u32[]{:S(2)}) copy-start(f32[1024]{0:T(1024)} %param.24) | copy-start | bytes 12292
  425.1 3.6 copy-start.79
  715.1 3.9 copy-start.35
  719.0 2.9 copy-start.34
  719.0 4.4 copy-start.1
  (42 other events, 63.0 us)
Sparse Core Ops, SparseCore 0:
  298.2 344.0 all-reduce.10
